TPU v7x, 32 devices: a whole 2x2x4 slice. The times are simulated.
32 devices in a mesh: dp: 8 (over z, x), group: 4 (over y, core).
Axes of the slice: x: 2, y: 2, z: 4, core: 2. Of those that a mesh axis runs over, the one named last changes fastest.
Arguments:
- tokens: bfloat16 [24576, 1024], P(('dp', 'group')), may hold values from -6 to 6
- segments: int32 [24576], P('dp'), may hold values from 0 to 2, as said below
- cotangent: bfloat16 [24576, 1024], P(('dp', 'group')), may hold values from -6 to 6
- mixer_master: float32 [1024, 4096], P(('dp', 'group')), may hold values from -0.1875 to 0.1875
- mixer_first: float32 [1024, 4096], P(('dp', 'group')), may hold values from -78.383675 to 78.383675
- mixer_second: float32 [1024, 4096], P(('dp', 'group')), may hold values from 1292.6976 to 5160.96
- ffn_master: float32 [1024, 3, 4608], P(('dp', 'group')), may hold values from -0.1875 to 0.1875
- ffn_first: float32 [1024, 3, 4608], P(('dp', 'group')), may hold values from -39.191837 to 39.191837
- ffn_second: float32 [1024, 3, 4608], P(('dp', 'group')), may hold values from 319.488 to 1302.528
- small_master: float32 [5, 1024], P(None, 'group'), may hold values from 0.25 to 1.75
- small_first: float32 [5, 1024], P(None, 'group'), may hold values from -78.383675 to 78.383675
- small_second: float32 [5, 1024], P(None, 'group'), may hold values from 1292.6976 to 5160.96
Outputs:
- block_out: float32 [24576, 1024], P(('dp', 'group'))
- tokens_grad: float32 [24576, 1024], P(('dp', 'group'))
- mixer_first_new: float32 [1024, 4096], P(('dp', 'group'))
- mixer_second_new: float32 [1024, 4096], P(('dp', 'group'))
- mixer_new: float32 [1024, 4096], P(('dp', 'group'))
- ffn_first_new: float32 [1024, 3, 4608], P(('dp', 'group'))
- ffn_second_new: float32 [1024, 3, 4608], P(('dp', 'group'))
- ffn_new: float32 [1024, 3, 4608], P(('dp', 'group'))
- small_first_new: float32 [5, 1024], P(None, 'group')
- small_second_new: float32 [5, 1024], P(None, 'group')
- small_new: float32 [5, 1024], P(None, 'group')
Inputs may be any that keep to these rules, and one draw needn't show every extreme that they name: `segments`: within each sequence of 3072 tokens the numbers are 0, 1, 2 in order; document 1 begins within the first 384 tokens and ends within the last 384 tokens.
All inputs are finite; a program needn't handle non-finite values.
Results may differ from a plain program's by a relative error of at most 0.022.
Values may be sent and summed in bfloat16 or wider, within the bound.
No kernel may reach another device: no remote copies, remote signals or barrier semaphores. Data moves between devices by JAX's collectives and lax.ppermute only.
A program may use at most 256 MiB of HBM per device.

v0:
```python
import jax
import jax.numpy as jnp
from jax import lax
from jax.sharding import PartitionSpec as P

STEP = 10


norm_eps = 1e-06
beta_one = 0.9
beta_two = 0.95
adam_eps = 1e-08
decay_rate = 0.1
rate_matrix = 0.02
rate_small = 1.0


def shifted(block, axis, distance):
    devices = range(lax.axis_size(axis))
    route = [(i - distance, i) for i in devices if i - distance in devices]
    return lax.ppermute(block, axis, route)


def norm_forward(values, gain):
    scale = lax.rsqrt(jnp.mean(values * values, axis=-1, keepdims=True) + norm_eps)
    normed = values * scale
    return (normed, scale, normed * gain)


def norm_backward(grad_normed, normed, scale, gain):
    grad_hat = grad_normed * gain
    grad_in = scale * (grad_hat - normed * jnp.mean(grad_hat * normed, axis=-1, keepdims=True))
    return (grad_in, jnp.sum(grad_normed * normed, axis=0))


def contract_rows(left, right):
    return lax.dot_general(
        left, right, (((0,), (0,)), ((), ())), preferred_element_type=jnp.float32
    )


def contract_cols(left, right):
    return lax.dot_general(
        left, right, (((1,), (1,)), ((), ())), preferred_element_type=jnp.float32
    )


def adamw(master, first, second, grad, rate, decay):
    first_new = beta_one * first + (1.0 - beta_one) * grad
    second_new = beta_two * second + (1.0 - beta_two) * grad * grad
    fix_one = 1.0 - beta_one**STEP
    fix_two = 1.0 - beta_two**STEP
    direction = first_new / fix_one / (jnp.sqrt(second_new / fix_two) + adam_eps)
    return (first_new, second_new, master - rate * (direction + decay * master))


def local(
    tokens,
    segments,
    cotangent,
    mixer_master,
    mixer_first,
    mixer_second,
    ffn_master,
    ffn_first,
    ffn_second,
    small_master,
    small_first,
    small_second,
):
    width = tokens.shape[1]
    length = tokens.shape[0]
    hidden_width = ffn_master.shape[2]
    owned_rows = mixer_master.shape[0]
    group_count = lax.axis_size("group")
    mixer_low = mixer_master.astype(jnp.bfloat16)
    ffn_low = ffn_master.astype(jnp.bfloat16)
    small_all = lax.all_gather(
        small_master.astype(jnp.bfloat16), "group", axis=1, tiled=True
    ).astype(jnp.float32)
    sectioned = (
        lax.all_gather(mixer_low, "group", axis=0, tiled=True),
        lax.all_gather(ffn_low, "group", axis=0, tiled=True),
    )
    mixer_all, ffn_all = (
        lax.all_gather(sectioned[0], "dp", axis=0, tiled=True),
        lax.all_gather(sectioned[1], "dp", axis=0, tiled=True),
    )
    w_in = mixer_all[:, : 3 * width]
    w_out = mixer_all[:, 3 * width :]
    w_gate = ffn_all[:, 0, :]
    w_up = ffn_all[:, 1, :]
    w_down = ffn_all[:, 2, :]
    block_start = lax.axis_index("group") * length
    sentinel = jnp.full((2,), -1, jnp.int32)
    docs_before = lax.dynamic_slice_in_dim(
        jnp.concatenate([sentinel, segments]), block_start, length + 2
    )
    docs_after = lax.dynamic_slice_in_dim(
        jnp.concatenate([segments, sentinel]), block_start, length + 2
    )
    own_docs = docs_before[2:]
    inputs = tokens.astype(jnp.float32)
    first_normed, first_scale, first_pre = norm_forward(inputs, small_all[0])
    first_in = first_pre.astype(jnp.bfloat16)
    projected = jnp.dot(first_in, w_in, preferred_element_type=jnp.float32)
    first_gate = projected[:, :width]
    output_gate = projected[:, width : 2 * width]
    values_in = projected[:, 2 * width :]
    gated_values = (first_gate * values_in).astype(jnp.bfloat16)
    rim_rows = shifted(gated_values[length - 2 :], "group", 1)
    padded = jnp.concatenate([rim_rows, gated_values], axis=0).astype(jnp.float32)
    convolved = jnp.zeros((length, width), jnp.float32)
    masks = []
    for offset in range(3):
        same = (docs_before[2 - offset : 2 - offset + length] == own_docs).astype(jnp.float32)[
            :, None
        ]
        masks.append(same)
        convolved = (
            convolved + small_all[2 + offset] * padded[2 - offset : 2 - offset + length] * same
        )
    mixer_in = (output_gate * convolved).astype(jnp.bfloat16)
    mixed = jnp.dot(mixer_in, w_out, preferred_element_type=jnp.float32)
    residual = inputs + mixed
    second_normed, second_scale, second_pre = norm_forward(residual, small_all[1])
    second_in = second_pre.astype(jnp.bfloat16)
    ffn_gate = jnp.dot(second_in, w_gate, preferred_element_type=jnp.float32)
    ffn_up = jnp.dot(second_in, w_up, preferred_element_type=jnp.float32)
    sigmoid_gate = jax.nn.sigmoid(ffn_gate)
    swish = ffn_gate * sigmoid_gate
    hidden_act = (swish * ffn_up).astype(jnp.bfloat16)
    block_out = residual + contract_cols(hidden_act, w_down)
    grad_act = jnp.dot(cotangent, w_down, preferred_element_type=jnp.float32)
    grad_gate = (grad_act * ffn_up * sigmoid_gate * (1.0 + ffn_gate * (1.0 - sigmoid_gate))).astype(
        jnp.bfloat16
    )
    grad_up = (grad_act * swish).astype(jnp.bfloat16)
    grad_second = contract_cols(grad_gate, w_gate) + contract_cols(grad_up, w_up)
    grad_resid_norm, gain_two = norm_backward(
        grad_second, second_normed, second_scale, small_all[1]
    )
    grad_resid = cotangent.astype(jnp.float32) + grad_resid_norm
    grad_mixed = grad_resid.astype(jnp.bfloat16)
    grad_mixer_in = contract_cols(grad_mixed, w_out)
    grad_conv = (grad_mixer_in * output_gate).astype(jnp.bfloat16)
    grad_output_gate = grad_mixer_in * convolved
    rim_ahead = shifted(grad_conv[:2], "group", -1)
    ahead = jnp.concatenate([grad_conv, rim_ahead], axis=0).astype(jnp.float32)
    grad_conv_full = ahead[:length]
    grad_gated = jnp.zeros((length, width), jnp.float32)
    tap_terms = []
    for offset in range(3):
        same_ahead = (docs_after[offset : offset + length] == own_docs).astype(jnp.float32)[:, None]
        grad_gated = (
            grad_gated + small_all[2 + offset] * ahead[offset : offset + length] * same_ahead
        )
        tap_terms.append(
            jnp.sum(
                grad_conv_full * padded[2 - offset : 2 - offset + length] * masks[offset], axis=0
            )
        )
    grad_projected = jnp.concatenate(
        [grad_gated * values_in, grad_output_gate, grad_gated * first_gate], axis=1
    ).astype(jnp.bfloat16)
    grad_first = contract_cols(grad_projected, w_in)
    grad_input_norm, gain_one = norm_backward(grad_first, first_normed, first_scale, small_all[0])
    tokens_grad = grad_resid + grad_input_norm

    def term_maker(first_cols, mixer_cols, second_cols, cotangent_cols):

        def weight_terms(start, count):
            return jnp.concatenate(
                [
                    contract_rows(first_cols, grad_projected),
                    contract_rows(mixer_cols, grad_mixed),
                    contract_rows(second_cols, grad_gate),
                    contract_rows(second_cols, grad_up),
                    contract_rows(cotangent_cols, hidden_act),
                ],
                axis=1,
            )

        return weight_terms

    weight_terms = term_maker(first_in, mixer_in, second_in, cotangent)
    partial_sum = lax.psum_scatter(
        weight_terms(jnp.int32(0), owned_rows * group_count * lax.axis_size("dp")).astype(
            jnp.bfloat16
        ),
        "dp",
        scatter_dimension=0,
        tiled=True,
    )
    summed = lax.psum_scatter(partial_sum, "group", scatter_dimension=0, tiled=True).astype(
        jnp.float32
    )
    mixer_grad = summed[:, : 4 * width]
    ffn_grad = summed[:, 4 * width :].reshape(owned_rows, 3, hidden_width)
    small_term = jnp.stack([gain_one, gain_two] + tap_terms, axis=0)
    small_part = lax.psum_scatter(small_term, "group", scatter_dimension=1, tiled=True)
    small_grad = lax.psum(small_part, "dp")
    mixer_f, mixer_s, mixer_n = adamw(
        mixer_master, mixer_first, mixer_second, mixer_grad, rate_matrix, decay_rate
    )
    ffn_f, ffn_s, ffn_n = adamw(
        ffn_master, ffn_first, ffn_second, ffn_grad, rate_matrix, decay_rate
    )
    small_f, small_s, small_n = adamw(
        small_master, small_first, small_second, small_grad, rate_small, 0.0
    )
    return (
        block_out,
        tokens_grad,
        mixer_f,
        mixer_s,
        mixer_n,
        ffn_f,
        ffn_s,
        ffn_n,
        small_f,
        small_s,
        small_n,
    )


def solution(mesh):
    in_specs = (
        P(("dp", "group"), None),
        P("dp"),
        P(("dp", "group"), None),
        P(("dp", "group"), None),
        P(("dp", "group"), None),
        P(("dp", "group"), None),
        P(("dp", "group"), None, None),
        P(("dp", "group"), None, None),
        P(("dp", "group"), None, None),
        P(None, "group"),
        P(None, "group"),
        P(None, "group"),
    )
    out_specs = (
        P(("dp", "group"), None),
        P(("dp", "group"), None),
        P(("dp", "group"), None),
        P(("dp", "group"), None),
        P(("dp", "group"), None),
        P(("dp", "group"), None, None),
        P(("dp", "group"), None, None),
        P(("dp", "group"), None, None),
        P(None, "group"),
        P(None, "group"),
        P(None, "group"),
    )
    return jax.shard_map(local, mesh=mesh, in_specs=in_specs, out_specs=out_specs, check_vma=False)
```

profile of v0, /device:TPU:0, one launch (start us, length us, event | category | flops | bytes accessed | tf_op | source)
XLA Modules:
  0.0 1553.1 jit_solution(8765176692095704148)
XLA Ops:
  7.2 1.8 convert_element_type.78
  9.1 2.5 convert_element_type.85
  11.6 18.0 %all-gather.5.cloned.1.call-done = bf16[128,4096]{1,0:T(8,128)(2,1)} async-done(((bf16[32,4096]{1,0:T(8,128)(2,1)}), bf16[128,4096]{1,0:T(8,128)(2,1)}) %all-gather.5.cloned.1.call-update) | async-done | bytes 1048592 | tf_op jit(solution)/shard_map/all_gather | solution.py:82
  29.7 32.9 %all-gather.9.cloned.1.call-done = bf16[128,3,4608]{2,0,1:T(8,128)(2,1)} async-done(((bf16[32,3,4608]{2,0,1:T(8,128)(2,1)}), bf16[128,3,4608]{2,0,1:T(8,128)(2,1)}) %all-gather.9.cloned.1.call-update) | async-done | bytes 3538960 | tf_op jit(solution)/shard_map/all_gather | solution.py:83
  62.6 5.2 all_gather.15
  68.4 121.3 %all-gather.7.cloned.1.call-done = bf16[1024,4096]{1,0:T(8,128)(2,1)} async-done(((bf16[128,4096]{1,0:T(8,128)(2,1)}), bf16[1024,4096]{1,0:T(8,128)(2,1)}) %all-gather.7.cloned.1.call-update) | async-done | bytes 8388624 | tf_op jit(solution)/shard_map/all_gather | solution.py:86
  189.6 7.4 fusion.11
  197.0 0.5 multiply_convert_fusion.9
  197.6 1.5 collective-permute-start
  200.7 2.8 multiply_convert_fusion.8
  203.5 4.1 multiply_reduce_fusion.5
  207.6 1.6 copy-done.1
  209.2 1.5 multiply_convert_fusion.7
  210.7 518.0 %all-gather.11.cloned.1.call-done = bf16[1024,3,4608]{2,0,1:T(8,128)(2,1)} async-done(((bf16[128,3,4608]{2,0,1:T(8,128)(2,1)}), bf16[1024,3,4608]{2,0,1:T(8,128)(2,1)}) %all-gather.11.cloned.1.call-update) | async-done | bytes 28311568 | tf_op jit(solution)/shard_map/all_gather | solution.py:87
  728.7 14.6 fusion.6
  743.3 13.9 fusion.4
  757.2 25.4 %multiply_convert_fusion = (bf16[768,4608]{1,0:T(8,128)(2,1)}, bf16[768,4608]{1,0:T(8,128)(2,1)}, bf16[768,4608]{1,0:T(8,128)(2,1)}) fusion(f32[768,4608]{1,0:T(8,128)} %fusion.4, f32[768,4608]{1,0:T(8,128)} %fusion.6, bf16[768,1024]{1,0:T(8,128)(2,1)S(1)} %copy-done.22, bf16[1024,3,4608]{2,0,1:T(8,128)(2,1)} %all-gather.11.cloned.1.call-done), kind=kOutput, calls=%fused_computation | convolution fusion | flops 7300841472 | bytes 60555264 | tf_op jit(solution)/shard_map/dot_general | solution.py:134
  782.6 12.5 fusion.3
  795.2 12.8 multiply_reduce_fusion.3
  808.0 0.8 multiply_add_fusion
  808.8 4.6 fusion.30
  813.5 4.5 multiply_convert_fusion.4
  817.9 1.1 copy-done.10
  819.1 1.3 collective-permute-start.1
  820.4 3.2 convolution_convert_fusion.3
  823.6 4.4 copy.38
  828.0 1.8 maximum_convert_fusion.1
  829.8 4.5 multiply_reduce_fusion
  834.4 3.1 multiply_convert_fusion.3
  837.7 7.8 convert_dynamic-update-slice_fusion
  845.5 1.6 constant_dynamic-update-slice_fusion
  847.6 9.8 fusion.2
  857.5 9.8 fusion.1
  867.3 10.0 bitcast_dynamic-update-slice_fusion
  877.3 10.7 fusion.22
  888.0 0.6 stack.23
  888.7 578.1 %reduce-scatter.4.cloned.1.call-done = bf16[128,17920]{1,0:T(8,128)(2,1)} async-done(((bf16[1024,17920]{1,0:T(8,128)(2,1)}), bf16[128,17920]{1,0:T(8,128)(2,1)}) %reduce-scatter.4.cloned.1.call-update) | async-done | bytes 4587536 | tf_op jit(solution)/shard_map/reduce_scatter | solution.py:187
  1467.0 13.4 fusion.28
  1480.5 2.5 fusion.21
  1482.9 5.3 reduce-scatter.8.cloned.1.call-done
  1488.2 21.9 %psum.7 = f32[5,256]{1,0:T(8,128)S(1)} all-reduce(f32[5,256]{1,0:T(8,128)} %reduce-scatter.8.cloned.1.call-done), channel_id=1, replica_groups=mesh['dp'=8,'group'=4] {'dp'}, use_global_device_ids=true, to_apply=%region_12.0 | all-reduce | flops 1280 | bytes 10240 | tf_op jit(solution)/shard_map/psum | solution.py:202
  1510.2 0.6 add_subtract_fusion
  1510.8 27.2 %reduce-scatter.6.cloned.1.call-done = bf16[32,17920]{1,0:T(8,128)(2,1)} async-done(((bf16[128,17920]{1,0:T(8,128)(2,1)}), bf16[32,17920]{1,0:T(8,128)(2,1)}) %reduce-scatter.6.cloned.1.call-update) | async-done | bytes 1146896 | tf_op jit(solution)/shard_map/reduce_scatter | solution.py:195
  1538.0 1.5 convert_element_type.96
  1539.6 1.4 multiply_subtract_fusion.1
  1541.6 0.5 copy-done.17
  1542.1 0.5 copy-done.18
  1542.7 3.3 multiply_subtract_fusion
  (118 shorter events, 3.9 us)
Async XLA Ops:
  7.2 22.4 %all-gather.5.cloned.1.call-start = ((), (), s32[]{:S(2)}) async-start(), calls=%async_computation.3 | async-start | bytes 1310720 | tf_op jit(solution)/shard_map/all_gather | solution.py:82
  9.0 53.5 %all-gather.9.cloned.1.call-start = ((), (), s32[]{:S(2)}) async-start(), calls=%async_computation.5 | async-start | bytes 4423680 | tf_op jit(solution)/shard_map/all_gather | solution.py:83
  11.5 51.1 %copy-start.30 = (f32[5,256]{1,0:T(8,128)S(1)}, f32[5,256]{1,0:T(8,128)}, u32[]{:S(2)}) copy-start(f32[5,256]{1,0:T(8,128)} %param.21) | copy-start | bytes 15364
  11.5 56.3 %copy-start.36 = (s32[3072]{0:T(1024)S(1)}, s32[3072]{0:T(1024)}, u32[]{:S(2)}) copy-start(s32[3072]{0:T(1024)} %param.13) | copy-start | bytes 36868
  11.6 56.4 %copy-start.11 = (bf16[768,1024]{1,0:T(8,128)(2,1)S(1)}, bf16[768,1024]{1,0:T(8,128)(2,1)}, u32[]{:S(2)}) copy-start(bf16[768,1024]{1,0:T(8,128)(2,1)} %param.12) | copy-start | bytes 4718596
  11.6 178.1 %all-gather.7.cloned.1.call-start = ((), (), s32[]{:S(2)}) async-start(), calls=%async_computation.4 | async-start | bytes 9437184 | tf_op jit(solution)/shard_map/all_gather | solution.py:86
  29.6 699.0 %all-gather.11.cloned.1.call-start = ((), (), s32[]{:S(2)}) async-start(), calls=%async_computation.6 | async-start | bytes 31850496 | tf_op jit(solution)/shard_map/all_gather | solution.py:87
  62.6 1404.3 %reduce-scatter.4.cloned.1.call-start = ((), (), s32[]{:S(2)}) async-start(), calls=%async_computation.7 | async-start | bytes 41287680 | tf_op jit(solution)/shard_map/reduce_scatter | solution.py:187
  68.3 128.7 %copy-start.34 = (f32[768]{0:T(1024)}, f32[768]{0:T(1024)S(1)}, u32[]{:S(2)}) copy-start(f32[768]{0:T(1024)S(1)} %add_rsqrt_fusion.1) | copy-start | bytes 9220
  68.3 128.7 %copy-start.32 = (f32[1,1024]{1,0:T(1,128)}, f32[1,1024]{1,0:T(1,128)S(1)}, u32[]{:S(2)}) copy-start(f32[1,1024]{1,0:T(1,128)S(1)} %get-tuple-element.53) | copy-start | bytes 12292
  197.0 3.6 copy-start
  197.6 2.1 collective-permute-start
  203.5 4.1 copy-start.26
  728.7 14.6 copy-start.20
  743.3 13.9 copy-start.22
  782.6 12.6 copy-start.2
  808.8 11.6 copy-start.4
  808.8 4.6 copy-start.6
  813.4 6.9 copy-start.27
  819.1 8.9 collective-permute-start.1
  834.3 3.2 copy-start.25
  834.3 3.2 copy-start.13
  834.3 3.4 copy-start.19
  834.3 3.4 copy-start.33
  834.3 3.4 copy-start.35
  834.4 12.7 slice-start.2
  837.4 8.0 copy-start.24
  837.7 7.8 copy-start.7
  837.7 9.4 slice-start.3
  845.5 11.9 slice-start
  847.6 9.9 slice-start.1
  847.6 19.7 %slice-start.4 = ((s8[7077888]{0:T(1024)(128)(4,1)}), s8[2883584]{0:T(1024)(128)(4,1)S(1)}, s32[]{:S(2)}) async-start(s8[7077888]{0:T(1024)(128)(4,1)} %bitcast.77), calls=%async_computation.14 | async-start | bytes 5767168
  857.4 9.8 copy-start.23
  857.4 9.8 slice-start.5
  877.3 611.0 %reduce-scatter.8.cloned.1.call-start = ((), (), s32[]{:S(2)}) async-start(), calls=%async_computation.9 | async-start | bytes 40960 | tf_op jit(solution)/shard_map/reduce_scatter | solution.py:201
  888.0 578.9 %copy-start.3 = (f32[768,1024]{1,0:T(8,128)S(1)}, f32[768,1024]{1,0:T(8,128)}, u32[]{:S(2)}) copy-start(f32[768,1024]{1,0:T(8,128)} %copy-done.1) | copy-start | bytes 9437188
  888.7 649.3 %reduce-scatter.6.cloned.1.call-start = ((), (), s32[]{:S(2)}) async-start(), calls=%async_computation.8 | async-start | bytes 5734400 | tf_op jit(solution)/shard_map/reduce_scatter | solution.py:195
  1466.9 13.5 copy-start.5
  1466.9 13.5 copy-start.14
  1467.0 13.5 copy-start.15
  1480.4 29.8 %copy-start.31 = (f32[5,256]{1,0:T(8,128)S(1)}, f32[5,256]{1,0:T(8,128)}, u32[]{:S(2)}) copy-start(f32[5,256]{1,0:T(8,128)} %param.21) | copy-start | bytes 15364
  1480.4 29.8 %copy-start.37 = (f32[5,256]{1,0:T(8,128)S(1)}, f32[5,256]{1,0:T(8,128)}, u32[]{:S(2)}) copy-start(f32[5,256]{1,0:T(8,128)} %param.23) | copy-start | bytes 15364
  1480.4 29.8 %copy-start.38 = (f32[5,256]{1,0:T(8,128)S(1)}, f32[5,256]{1,0:T(8,128)}, u32[]{:S(2)}) copy-start(f32[5,256]{1,0:T(8,128)} %param.22) | copy-start | bytes 15364
  1482.9 56.6 %copy-start.16 = (f32[32,4096]{1,0:T(8,128)S(1)}, f32[32,4096]{1,0:T(8,128)}, u32[]{:S(2)}) copy-start(f32[32,4096]{1,0:T(8,128)} %param.15) | copy-start | bytes 1572868
  1482.9 56.6 %copy-start.28 = (f32[32,4096]{1,0:T(8,128)S(1)}, f32[32,4096]{1,0:T(8,128)}, u32[]{:S(2)}) copy-start(f32[32,4096]{1,0:T(8,128)} %param.17) | copy-start | bytes 1572868
  1482.9 56.6 %copy-start.29 = (f32[32,4096]{1,0:T(8,128)S(1)}, f32[32,4096]{1,0:T(8,128)}, u32[]{:S(2)}) copy-start(f32[32,4096]{1,0:T(8,128)} %param.16) | copy-start | bytes 1572868
  1538.0 3.0 copy-start.8
  1539.6 3.1 copy-start.18
  (6 other events, 12.4 us)
Sparse Core Ops, SparseCore 0:
  10.1 19.4 all-gather.4
  31.7 30.7 all-gather.8
  64.7 124.9 all-gather.6
  191.0 537.5 all-gather.10
  877.4 589.4 reduce-scatter.3
  1469.7 18.4 reduce-scatter.7
  1491.0 46.9 reduce-scatter.5
where the time goes:
time: 1560 us; the launch traced here: 1550 us
  waiting for transfers between devices  1300 us (83%)
  matrix products  160 us (10%)
  other arithmetic  34 us (2%)
  blocking collectives  27.1 us (2%)
    reduce_scatter x1, waiting for transfers between devices, local(): lax.psum_scatter(weight_terms(jnp.int32(0), owned_rows * group_count * la...  578 us
    all_gather x1, waiting for transfers between devices, local(): lax.all_gather(sectioned[1], 'dp', axis=0, tiled=True)  518 us
    all_gather x1, waiting for transfers between devices, local(): lax.all_gather(sectioned[0], 'dp', axis=0, tiled=True)  121 us
    dot_general x5, matrix products, contract_cols(): lax.dot_general(left, right, (((1,), (1,)), ((), ())), preferred_element_...  54 us
    dot_general x5, matrix products, contract_rows(): lax.dot_general(left, right, (((0,), (0,)), ((), ())), preferred_element_...  40.6 us
    all_gather x1, waiting for transfers between devices, local(): lax.all_gather(ffn_low, 'group', axis=0, tiled=True)  32.9 us
  transfers between devices with their start and end apart: 9, of which 8 were waited for; matrix products, arithmetic and copies ran while one was open for 4% of the time, Pallas kernels for 0%

commit v1 on v0

v1 whole, which is shorter than its diff:
```python
import functools

import jax
import jax.numpy as jnp
from jax import lax
from jax.experimental import pallas as pl
from jax.experimental.pallas import tpu as pltpu
from jax.sharding import PartitionSpec as P

STEP = 10

norm_eps = 1e-06
beta_one = 0.9
beta_two = 0.95
adam_eps = 1e-08
decay_rate = 0.1
rate_matrix = 0.02
rate_small = 1.0

MIB = 1 << 20
ORDER = ((0, 5), (0, 10), (3, 10), (29, 30), (26, 34), (37, 43), (40, 43), (39, 46), (50, 51), (40, 56), (44, 57), (40, 63), (61, 65), (56, 66), (62, 70), (53, 74), (68, 74), (72, 75), (79, 83))
OFF = ((3, 2), (4, 0), (5, 0), (12, 0), (15, 2), (17, 0), (19, 0))
trace = None
VMEM = 60
WEIGHT = 0.001
BF16 = jnp.bfloat16
F32 = jnp.float32
GROUP = 4
NEAR, FAR = 1, 2


def shape_of(shape, dtype):
    return jax.ShapeDtypeStruct(tuple(shape), dtype)


def dot_rows(left, right):
    return lax.dot_general(left, right, (((0,), (0,)), ((), ())), preferred_element_type=F32)


def dot_cols(left, right):
    return lax.dot_general(left, right, (((1,), (1,)), ((), ())), preferred_element_type=F32)


def dot(left, right):
    return jnp.dot(left, right, preferred_element_type=F32)


def adamw(master, first, second, grad, rate, decay):
    first_new = beta_one * first + (1.0 - beta_one) * grad
    second_new = beta_two * second + (1.0 - beta_two) * grad * grad
    fix_one = 1.0 - beta_one**STEP
    fix_two = 1.0 - beta_two**STEP
    direction = first_new / fix_one / (jnp.sqrt(second_new / fix_two) + adam_eps)
    return (first_new, second_new, master - rate * (direction + decay * master))


class Trace:
    def __init__(self):
        self.results = []
        self.holds = 0

    def ready(self, operand):
        step = len(self.results)
        earlier = [self.results[j] for j, i in ORDER if i == step and j < step]
        return lax.optimization_barrier([operand] + earlier)[0] if earlier else operand

    def done(self, results):
        self.results.append(jax.tree.leaves(results)[0])
        return results


def swapped(block, axis, distance):
    pairs = [(i, i ^ distance) for i in range(lax.axis_size(axis))]
    return trace.done(lax.ppermute(trace.ready(block), axis, pairs))


def after(values, *others):
    hold = trace.holds
    trace.holds += 1
    others = tuple(o for j, o in enumerate(others) if (hold, j) not in OFF)
    return lax.optimization_barrier((values,) + others)[0] if others else values


def call(
    kernel, name, out_shape, *, where, grid=(), in_specs, out_specs, scratch=(), flops, moved, aliases={}
):
    run = pl.pallas_call(
        kernel,
        out_shape=out_shape,
        grid_spec=pltpu.PrefetchScalarGridSpec(
            num_scalar_prefetch=1,
            grid=grid,
            in_specs=in_specs,
            out_specs=out_specs,
            scratch_shapes=scratch,
        ),
        compiler_params=pltpu.CompilerParams(
            vmem_limit_bytes=VMEM * MIB,
            dimension_semantics=("arbitrary",) * len(grid) if grid else None,
        ),
        cost_estimate=pl.CostEstimate(
            flops=int(flops * WEIGHT), bytes_accessed=int(moved * WEIGHT), transcendentals=0
        ),
        input_output_aliases=aliases,
        name=name,
    )
    return lambda first, *rest: trace.done(run(where, trace.ready(first), *rest))


def whole(array):
    rank = len(array.shape)
    return pl.BlockSpec(tuple(array.shape), lambda *_: (0,) * rank)


def wholes(arrays):
    return [whole(a) for a in arrays]


def untouched():
    return pl.BlockSpec(memory_space=pl.ANY)


def send_kernel(where, mixer, ffn, small, *outs, part, hpart, chunks):
    me = where[0]
    base = 4 * part
    last = base + 3 * hpart
    for k in range(GROUP):
        out = outs[k]
        for j in range(4):
            start = pl.multiple_of((me ^ k) * part + j * GROUP * part, part)
            out[:, j * part : (j + 1) * part] = mixer[:, pl.ds(start, part)].astype(BF16)
        for first, size in chunks:
            start = pl.multiple_of((me ^ k) * hpart + first, 128)
            for j in range(3):
                at = base + 3 * first + j * size
                out[:, at : at + size] = ffn[j, :, pl.ds(start, size)].astype(BF16)
        pad = jnp.zeros((out.shape[0] - small.shape[0], part), F32)
        out[:, last:] = jnp.concatenate([small[...], pad], axis=0).astype(BF16)


def take_kernel(where, *refs, part, hpart, chunks):
    blocks, (mixer, small), ffns = refs[:GROUP], refs[GROUP : GROUP + 2], refs[GROUP + 2 :]
    base = 4 * part
    last = base + 3 * hpart
    for k in range(GROUP):
        source = where[0] ^ k
        mixer[source] = blocks[k][:, :base]
        for out, (first, size) in zip(ffns, chunks):
            out[source] = blocks[k][:, base + 3 * first : base + 3 * (first + size)]
        small[:, pl.ds(pl.multiple_of(source * part, part), part)] = blocks[k][:, last:].astype(F32)[
            :8
        ]


def out_stack_kernel(where, *refs, start, size):
    pieces, (out, sems) = refs[:-2], refs[-2:]
    fetch_rows(where, pieces, out, sems, start, size)


def fetch_rows(where, pieces, target, sems, first, cols):
    rows = pieces[0].shape[0]
    copies = [
        pltpu.make_async_copy(
            piece.at[:, pl.ds(first, cols)],
            target.at[pl.ds(pl.multiple_of((where[1] ^ e) * rows, 32), rows), :],
            sems.at[e],
        )
        for e, piece in enumerate(pieces)
    ]
    for copy in copies:
        copy.start()
    for copy in copies:
        copy.wait()


def same_document(where, place, lag):
    same = place >= lag
    for begin in (where[2], where[3]):
        same = jnp.logical_and(same, jnp.logical_or(place < begin, place >= begin + lag))
    return same


def mixer_in_kernel(where, *refs, count, tiles, part):
    tokens, small, refs = refs[:GROUP], refs[GROUP], refs[GROUP + 1 :]
    pieces, refs = refs[:count], refs[count:]
    first_in, projected, convolved, mixer_in, w_in, held, carry, sems = refs
    step = pl.program_id(0)
    me = where[0]

    @pl.when(step == 0)
    def _():
        fetch_rows(where, pieces, w_in, sems, 0, 3 * part)
        carry[...] = jnp.zeros_like(carry)

    for k in range(GROUP):

        @pl.when((step // tiles) ^ me == k)
        def _(k=k):
            held[...] = tokens[k][...]

    inputs = held[...].astype(F32)
    scale = lax.rsqrt(jnp.mean(inputs * inputs, axis=-1, keepdims=True) + norm_eps)
    normed = (inputs * scale * small[0:1, :]).astype(BF16)
    first_in[...] = normed
    columns = dot(normed, w_in[...])
    projected[...] = columns
    gated = (columns[:, :part] * columns[:, 2 * part :]).astype(BF16).astype(F32)
    taps = small[2:5, pl.ds(pl.multiple_of(me * part, part), part)]
    row = lax.broadcasted_iota(jnp.int32, gated.shape, 0)
    before = carry[...]
    one = jnp.where(row == 0, before[7:8], pltpu.roll(gated, 1, 0))
    two = jnp.where(
        row == 0, before[6:7], jnp.where(row == 1, before[7:8], pltpu.roll(gated, 2, 0))
    )
    carry[...] = gated[gated.shape[0] - 8 :]
    place = row + step * gated.shape[0]
    one = jnp.where(same_document(where, place, 1), one, 0.0)
    two = jnp.where(same_document(where, place, 2), two, 0.0)
    mixed = taps[0:1] * gated + taps[1:2] * one + taps[2:3] * two
    convolved[...] = mixed
    mixer_in[...] = (columns[:, part : 2 * part] * mixed).astype(BF16)


def residual_kernel(where, *refs, tiles, part):
    tokens, mixer_in, refs = refs[:GROUP], refs[GROUP : 2 * GROUP], refs[2 * GROUP :]
    small, slices, refs = refs[0], refs[1 : 1 + GROUP], refs[1 + GROUP :]
    second_in, residual_out, mixer_own, w_out, held, inputs_held, sems = refs
    step = pl.program_id(0)
    columns = [pl.ds(pl.multiple_of((where[0] ^ k) * part, part), part) for k in range(GROUP)]

    @pl.when(step == 0)
    def _():
        copies = [
            pltpu.make_async_copy(slices[k], w_out.at[:, columns[k]], sems.at[k])
            for k in range(GROUP)
        ]
        for copy in copies:
            copy.start()
        for copy in copies:
            copy.wait()

    for k in range(GROUP):
        held[:, columns[k]] = mixer_in[k][...]

        @pl.when(step // tiles == k)
        def _(k=k):
            inputs_held[...] = tokens[k][...]

    residual = inputs_held[...].astype(F32) + dot(held[...], w_out[...])
    scale = lax.rsqrt(jnp.mean(residual * residual, axis=-1, keepdims=True) + norm_eps)
    second_in[...] = (residual * scale * small[1:2, :]).astype(BF16)

    @pl.when(step < tiles)
    def _():
        residual_out[...] = residual
        mixer_own[...] = held[...]


def ffn_kernel(where, *refs, tiles, part):
    many = 2 * tiles
    second_in, cots, source, refs = refs[0], refs[1 : 1 + many], refs[1 + many], refs[-11:]
    act_out, gate_out, up_out, cot_out, out_a, out_b, back_a, back_b, weights, held, sem = refs
    step = pl.program_id(0)

    @pl.when(step == 0)
    def _():
        copy = pltpu.make_async_copy(source, weights, sem)
        copy.start()
        copy.wait()

    for k in range(many):

        @pl.when(step == k)
        def _(k=k):
            held[...] = cots[k][...]

    normed = second_in[...]
    cotangent = held[...]
    cot_out[...] = cotangent
    for first in range(0, part, 256):
        size = min(256, part - first)
        gate = dot(normed, weights[:, first : first + size])
        up = dot(normed, weights[:, part + first : part + first + size])
        grad_act = dot(cotangent, weights[:, 2 * part + first : 2 * part + first + size])
        sig = 0.5 * jnp.tanh(0.5 * gate) + 0.5
        swish = gate * sig
        act_out[:, first : first + size] = (swish * up).astype(BF16)
        gate_out[:, first : first + size] = (
            grad_act * up * (sig * (1.0 + gate * (1.0 - sig)))
        ).astype(BF16)
        up_out[:, first : first + size] = (grad_act * swish).astype(BF16)
    out = dot_cols(act_out[...], weights[:, 2 * part :]).astype(BF16)
    back = (
        dot_cols(gate_out[...], weights[:, :part])
        + dot_cols(up_out[...], weights[:, part : 2 * part])
    ).astype(BF16)

    @pl.when(step < tiles)
    def _():
        out_a[...] = out
        back_a[...] = back

    @pl.when(step >= tiles)
    def _():
        out_b[...] = out
        back_b[...] = back


def weight_grad_kernel(where, *refs, lefts, rights, plan, rows, extra):
    left_refs, right_refs, refs = refs[:lefts], refs[lefts : lefts + rights], refs[lefts + rights :]
    if extra:
        (more,), refs = refs[:1], refs[1:]
    many = len(plan[0][2])
    outs, (left_held, right_held, total, sems) = refs[: 2 * many], refs[2 * many :]
    cols = total.shape[2]
    dp = where[1]

    def copies(at):
        left, left_start, sides, size = plan[at]
        slot = at % 2
        return [
            pltpu.make_async_copy(
                left_refs[left].at[pl.ds(left_start, size), :], left_held.at[slot], sems.at[0, slot]
            )
        ] + [
            pltpu.make_async_copy(
                right_refs[right].at[pl.ds(start, size), :],
                right_held.at[slot, m],
                sems.at[1 + m, slot],
            )
            for m, (right, start) in enumerate(sides)
        ]

    for copy in copies(0):
        copy.start()
    for at in range(len(plan)):
        if at + 1 < len(plan):
            for copy in copies(at + 1):
                copy.start()
        for copy in copies(at):
            copy.wait()
        left = left_held[at % 2]
        for m in range(many):
            part = dot_rows(left, right_held[at % 2, m])
            total[m] = part if at == 0 else total[m] + part
    for m in range(many):
        mine, theirs = outs[2 * m : 2 * m + 2]
        for j in range(mine.shape[0]):
            for target, side in ((mine, dp % 2), (theirs, 1 - dp % 2)):
                place = pl.multiple_of((2 * (j ^ (dp // 2)) + side) * rows, 32)
                target[j, :, :cols] = total[m, pl.ds(place, rows), :].astype(BF16)
                if extra:
                    target[j, :, cols:] = more[pl.ds(place, rows), :]


def out_grad_kernel(where, left, right, *refs, part):
    outs, held = refs[:GROUP], refs[GROUP]
    held[...] = dot_rows(left[...], right[...])
    for k in range(GROUP):
        outs[k][...] = held[:, pl.ds(pl.multiple_of((where[0] ^ k) * part, part), part)].astype(BF16)


def first_halve_kernel(where, mine_keep, mine_send, got_keep, got_send, keep, send):
    keep[...] = (mine_keep[...].astype(F32) + got_keep[...].astype(F32)).astype(BF16)
    send[...] = (mine_send[...].astype(F32) + got_send[...].astype(F32)).astype(BF16)


def halve_kernel(where, mine, got, keep, send):
    for j in range(keep.shape[0]):
        keep[j] = (mine[2 * j].astype(F32) + got[2 * j].astype(F32)).astype(BF16)
        send[j] = (mine[2 * j + 1].astype(F32) + got[2 * j + 1].astype(F32)).astype(BF16)


def finish_sum_kernel(where, *refs, terms, owned):
    outs, held = refs[-GROUP - 1 : -1], refs[-1]
    at = 0
    place = 0
    cols = held.shape[2]
    for many in terms:
        for first in range(0, refs[at].shape[1], cols):
            total = refs[at][:, first : first + cols].astype(F32)
            for other in refs[at + 1 : at + many]:
                total = total + other[:, first : first + cols].astype(F32)
            held[...] = total.reshape(held.shape)
            for k in range(GROUP):
                outs[k][place] = held[where[0] ^ k].astype(BF16)
            place += 1
        at += many


def residual_back_kernel(where, g0, g1, g2, residual, cotangent, small, w_out, *refs, part):
    grad_out, mixed_out, gain, outs, held = refs[0], refs[1], refs[2], refs[3:6], refs[6]
    grad = g0[...].astype(F32) + g1[...].astype(F32) + g2[...].astype(F32)
    values = residual[...]
    scale = lax.rsqrt(jnp.mean(values * values, axis=-1, keepdims=True) + norm_eps)
    normed = values * scale
    hat = grad * small[1:2, :]
    grad_in = cotangent[...].astype(F32) + scale * (
        hat - normed * jnp.mean(hat * normed, axis=-1, keepdims=True)
    )
    grad_out[...] = grad_in
    mixed = grad_in.astype(BF16)
    mixed_out[...] = mixed

    @pl.when(pl.program_id(0) == 0)
    def _():
        gain[...] = jnp.zeros_like(gain)

    gain[...] += jnp.sum(grad * normed, axis=0, keepdims=True)
    held[...] = dot_cols(mixed, w_out[...]).astype(BF16)
    for k in range(GROUP):
        columns = held[:, pl.ds(pl.multiple_of((where[0] ^ k) * part, part), part)]
        if k < FAR:
            outs[k][...] = columns
        else:
            outs[FAR][:, (k - FAR) * part : (k - FAR + 1) * part] = columns


def mixer_back_kernel(where, *refs, tiles, part):
    grads, tokens, refs = refs[:GROUP], refs[GROUP : 2 * GROUP], refs[2 * GROUP :]
    (projected, convolved, small, w_in), refs = refs[:4], refs[4:]
    grad_proj, tap_terms, gain, outs, (held, tokens_held, carry) = (
        refs[0],
        refs[1],
        refs[2],
        refs[3 : 3 + GROUP],
        refs[3 + GROUP :],
    )
    step = pl.program_id(0)
    me = where[0]
    which = ((pl.num_programs(0) - 1 - step) // tiles) ^ me

    @pl.when(step == 0)
    def _():
        carry[...] = jnp.zeros_like(carry)
        tap_terms[...] = jnp.zeros_like(tap_terms)
        gain[...] = jnp.zeros_like(gain)

    for k in range(GROUP):

        @pl.when(which == k)
        def _(k=k):
            held[...] = grads[k][...]
            tokens_held[...] = tokens[k][...]

    grad_mixer_in = held[...].astype(F32)
    first_gate = projected[:, :part]
    output_gate = projected[:, part : 2 * part]
    values_in = projected[:, 2 * part :]
    gated = (first_gate * values_in).astype(BF16).astype(F32)
    grad_conv = (grad_mixer_in * output_gate).astype(BF16).astype(F32)
    grad_output = grad_mixer_in * convolved[...]
    size = grad_conv.shape[0]
    row = lax.broadcasted_iota(jnp.int32, grad_conv.shape, 0)
    behind = carry[...]
    one = jnp.where(row == size - 1, behind[0:1], pltpu.roll(grad_conv, size - 1, 0))
    two = jnp.where(
        row == size - 1,
        behind[1:2],
        jnp.where(row == size - 2, behind[0:1], pltpu.roll(grad_conv, size - 2, 0)),
    )
    carry[...] = grad_conv[:8]
    place = row + (pl.num_programs(0) - 1 - step) * size
    last = pl.num_programs(0) * size
    one = jnp.where(jnp.logical_and(same_document(where, place + 1, 1), place + 1 < last), one, 0.0)
    two = jnp.where(jnp.logical_and(same_document(where, place + 2, 2), place + 2 < last), two, 0.0)
    taps = small[2:5, pl.ds(pl.multiple_of(me * part, part), part)]
    grad_gated = taps[0:1] * grad_conv + taps[1:2] * one + taps[2:3] * two
    tap_terms[0:1, :] += jnp.sum(grad_conv * gated, axis=0, keepdims=True)
    tap_terms[1:2, :] += jnp.sum(one * gated, axis=0, keepdims=True)
    tap_terms[2:3, :] += jnp.sum(two * gated, axis=0, keepdims=True)
    grad_proj[:, :part] = (grad_gated * values_in).astype(BF16)
    grad_proj[:, part : 2 * part] = grad_output.astype(BF16)
    grad_proj[:, 2 * part :] = (grad_gated * first_gate).astype(BF16)
    grad_first = dot_cols(grad_proj[...], w_in[...])
    inputs = tokens_held[...].astype(F32)
    scale = lax.rsqrt(jnp.mean(inputs * inputs, axis=-1, keepdims=True) + norm_eps)
    gain[...] += jnp.sum(grad_first * (inputs * scale), axis=0, keepdims=True)
    rounded = grad_first.astype(BF16)
    for k in range(GROUP):

        @pl.when(which == k)
        def _(k=k):
            outs[k][...] = rounded


def tokens_grad_kernel(where, g0, g1, g2, tokens, grad_resid, small, out):
    grad = g0[...].astype(F32) + g1[...].astype(F32) + g2[...].astype(F32)
    values = tokens[...].astype(F32)
    scale = lax.rsqrt(jnp.mean(values * values, axis=-1, keepdims=True) + norm_eps)
    normed = values * scale
    hat = grad * small[0:1, :]
    out[...] = grad_resid[...] + scale * (
        hat - normed * jnp.mean(hat * normed, axis=-1, keepdims=True)
    )


def mixer_adam_kernel(where, g0, g1, g2, g3, master, first, second, first_out, second_out, new_out, held, *, part):
    for k, grad in enumerate((g0, g1, g2, g3)):
        for j in range(4):
            start = (where[0] ^ k) * part + j * GROUP * part
            held[:, pl.ds(pl.multiple_of(start, part), part)] = grad[
                :, j * part : (j + 1) * part
            ].astype(F32)
    first_out[...], second_out[...], new_out[...] = adamw(
        master[...], first[...], second[...], held[...], rate_matrix, decay_rate
    )


def ffn_adam_kernel(where, g0, g1, g2, g3, master, first, second, first_out, second_out, new_out, held, *, part):
    for k, grad in enumerate((g0, g1, g2, g3)):
        start = pl.multiple_of((where[0] ^ k) * part, 128)
        held[:, pl.ds(start, part)] = grad[...].astype(F32)
    first_out[0], second_out[0], new_out[0] = adamw(
        master[0], first[0], second[0], held[...], rate_matrix, decay_rate
    )


def local(
    tokens,
    segments,
    cotangent,
    mixer_master,
    mixer_first,
    mixer_second,
    ffn_master,
    ffn_first,
    ffn_second,
    small_master,
    small_first,
    small_second,
):
    global trace
    trace = Trace()
    length, width = tokens.shape
    hidden = ffn_master.shape[2]
    owned = mixer_master.shape[0]
    count = lax.axis_size("dp")
    sequence = GROUP * length
    part = width // GROUP
    hpart = hidden // GROUP
    rows = GROUP * owned
    tile = length // 2
    tiles = length // tile
    steps = sequence // tile
    chunks = ((0, hpart),)
    where = jnp.stack([lax.axis_index("group"), lax.axis_index("dp")]).astype(jnp.int32)

    def group_gathered(own, *order, then=()):
        far = swapped(after(own, *order) if order else own, "group", FAR)
        near = swapped(own, "group", NEAR)
        return [own, near, far, swapped(after(far, *then) if then else far, "group", NEAR)]

    ffn_flat = ffn_master.transpose(1, 0, 2)
    send = [shape_of((owned, 4 * part + 3 * hpart + part), BF16)] * GROUP
    blocks = call(
        functools.partial(send_kernel, part=part, hpart=hpart, chunks=chunks),
        "send",
        send,
        where=where,
        in_specs=wholes([mixer_master, ffn_flat, small_master]),
        out_specs=wholes(send),
        flops=0,
        moved=owned * (width * 24 + hidden * 18),
    )(mixer_master, ffn_flat, small_master)
    blocks = [blocks[0]] + [swapped(blocks[k], "group", k) for k in range(1, GROUP)]
    take = [shape_of((GROUP, owned, 4 * part), BF16), shape_of((8, width), F32)]
    take += [shape_of((GROUP, owned, 3 * size), BF16) for _, size in chunks]
    mixer_rows, small_all, *ffn_rows = call(
        functools.partial(take_kernel, part=part, hpart=hpart, chunks=chunks),
        "take",
        take,
        where=where,
        in_specs=wholes(blocks),
        out_specs=wholes(take),
        flops=0,
        moved=owned * (width * 16 + hidden * 12),
    )(*blocks)
    far = count // 2

    def z_stages(own):
        pieces = {0: own}
        for e in sorted(range(2, count, 2), key=lambda e: (e.bit_count(), -e)):
            source = pieces[e & (e - 1)]
            pieces[e] = swapped(source, "dp", e & -e)
        return pieces

    mixer_own_rows = mixer_rows.reshape(rows, 4 * part)
    ffn_own_rows = [block.reshape(rows, block.shape[2]) for block in ffn_rows]
    mixer_z = z_stages(mixer_own_rows)
    mixer_near = swapped(mixer_own_rows, "dp", 1)
    mixer_z = lax.optimization_barrier([mixer_z[e] for e in range(2, count, 2)] + [mixer_near])
    mixer_z = mixer_z[: far - 1]
    ffn_cols = lax.all_gather(
        lax.optimization_barrier((ffn_own_rows[0], mixer_z[0], mixer_z[1]))[0], "dp", axis=0, tiled=True
    )
    mixer_x = [swapped(block, "dp", 1) for block in mixer_z]
    mixer_pieces = [mixer_own_rows, mixer_near]
    for block, other in zip(mixer_z, mixer_x):
        mixer_pieces += [block, other]

    tokens_far = swapped(after(tokens, *blocks[1:]), "group", FAR)
    tokens_of = [tokens, swapped(tokens, "group", NEAR), tokens_far]
    tokens_of += [swapped(after(tokens_far, *mixer_x), "group", NEAR)]

    begins = jnp.sum(
        segments[None, :] < jnp.array([[1], [2]], segments.dtype), axis=1, dtype=jnp.int32
    )
    where = jnp.concatenate([where, begins])

    out_stack = shape_of((width, part), BF16)
    out_stacked = call(
        functools.partial(out_stack_kernel, start=3 * part, size=part),
        "stack",
        out_stack,
        where=where,
        in_specs=[untouched()] * count,
        out_specs=whole(out_stack),
        scratch=[pltpu.SemaphoreType.DMA((count,))],
        flops=0,
        moved=width * part * 4,
    )(*mixer_pieces)
    out_slices = [out_stacked, swapped(out_stacked, "group", NEAR), swapped(out_stacked, "group", FAR)]

    def in_block(k, backward=False):
        def place(step, where):
            at = (steps - 1 - step) if backward else step
            return (jnp.clip(at - (where[0] ^ k) * tiles, 0, tiles - 1), 0)

        return place

    outs = [
        shape_of((sequence, width), BF16),
        shape_of((sequence, 3 * part), F32),
        shape_of((sequence, part), F32),
        shape_of((sequence, part), BF16),
        shape_of((width, 3 * part), BF16),
    ]
    forward = lambda s: pl.BlockSpec((tile, s.shape[1]), lambda i, w: (i, 0))
    first_in, projected, convolved, mixer_in, w_in = call(
        functools.partial(mixer_in_kernel, count=count, tiles=tiles, part=part),
        "mixer_in",
        outs,
        where=where,
        grid=(steps,),
        in_specs=[pl.BlockSpec((tile, width), in_block(k)) for k in range(GROUP)]
        + [whole(small_all)]
        + [untouched()] * count,
        out_specs=[forward(s) for s in outs[:4]] + [whole(outs[4])],
        scratch=[
            pltpu.VMEM((tile, width), BF16),
            pltpu.VMEM((8, part), F32),
            pltpu.SemaphoreType.DMA((count,)),
        ],
        flops=2 * sequence * width * 3 * part,
        moved=sequence * width * 8,
    )(*tokens_of, after(small_all, out_stacked), *mixer_pieces)
    out_slices += [swapped(out_slices[2], "group", NEAR)]
    mixer_in_of = group_gathered(after(mixer_in, out_slices[2]), then=out_slices)

    block_b = shape_of((length, width), BF16)
    outs = [
        shape_of((sequence, width), BF16),
        shape_of((length, width), F32),
        block_b,
        shape_of((width, width), BF16),
    ]
    own_block = pl.BlockSpec((tile, width), lambda i, w: (jnp.minimum(i, tiles - 1), 0))
    second_in, residual, mixer_own, w_out = call(
        functools.partial(residual_kernel, tiles=tiles, part=part),
        "residual",
        outs,
        where=where,
        grid=(steps,),
        in_specs=[
            pl.BlockSpec((tile, width), lambda i, w, k=k: (jnp.clip(i - k * tiles, 0, tiles - 1), 0))
            for k in range(GROUP)
        ]
        + [
            pl.BlockSpec((tile, part), lambda i, w: ((w[0] ^ (i // tiles)) * tiles + i % tiles, 0))
        ]
        * GROUP
        + [whole(small_all)]
        + [untouched()] * GROUP,
        out_specs=[forward(outs[0]), own_block, own_block, whole(outs[3])],
        scratch=[
            pltpu.VMEM((tile, width), BF16),
            pltpu.VMEM((tile, width), BF16),
            pltpu.SemaphoreType.DMA((GROUP,)),
        ],
        flops=2 * sequence * width * width,
        moved=sequence * width * 8,
    )(*tokens_of, *mixer_in_of, small_all, *out_slices)

    low = pl.BlockSpec((tile, width), lambda i, w: (jnp.minimum(i, tiles - 1), 0))
    high = pl.BlockSpec((tile, width), lambda i, w: (jnp.maximum(i - tiles, 0), 0))

    wholes_b = [shape_of((sequence, hpart), BF16)] * 3 + [shape_of((sequence, width), BF16)]

    def ffn_call(second_in, begin, cots, name, kept=()):
        at_tile = lambda s: pl.BlockSpec((tile, s.shape[1]), lambda i, w: (i + begin, 0))
        return call(
            functools.partial(ffn_kernel, tiles=tiles, part=hpart),
            name,
            wholes_b + [block_b] * 4,
            where=where,
            grid=(2 * tiles,),
            in_specs=[at_tile(second_in)]
            + [pl.BlockSpec((tile, width), lambda i, w, at=at: (at, 0)) for _, at in cots]
            + [untouched()] * (1 + len(kept)),
            out_specs=[at_tile(s) for s in wholes_b] + [low, high] * 2,
            scratch=[
                pltpu.VMEM((width, 3 * hpart), BF16),
                pltpu.VMEM((tile, width), BF16),
                pltpu.SemaphoreType.DMA(()),
            ],
            flops=24 * length * width * hpart,
            moved=2 * length * (hpart * 6 + width * 8) + width * hpart * 6,
            aliases={3 + len(cots) + j: j for j in range(len(kept))},
        )(second_in, *[cot for cot, _ in cots], ffn_cols, *kept)

    def for_far(mine, near):
        got = swapped(near, "group", NEAR)
        return (mine.astype(F32) + got.astype(F32)).astype(BF16)

    cotangent_near = swapped(cotangent, "group", NEAR)
    cotangent_far = swapped(after(cotangent, mixer_in_of[2]), "group", FAR)
    *kept, out_0, out_1, back_0, back_1 = ffn_call(
        second_in,
        0,
        [(block, at) for block in (cotangent, cotangent_near) for at in range(tiles)],
        "ffn_own",
    )
    cotangent_far = [
        cotangent_far,
        swapped(lax.optimization_barrier((cotangent_far, kept[0]))[0], "group", NEAR),
    ]
    hidden_act, grad_gate, grad_up, cotangents, out_2, out_3, back_2, back_3 = ffn_call(
        second_in,
        2 * tiles,
        [(block, at) for block in cotangent_far for at in range(tiles)],
        "ffn_far",
        kept,
    )
    back_near = swapped(back_1, "group", NEAR)
    back_sum = for_far(back_2, back_3)
    back_got = swapped(back_sum, "group", FAR)
    out_sum = for_far(out_2, out_3)
    out_near = swapped(out_1, "group", NEAR)

    def weight_grad(lefts, rights, plan, name, more=None):
        cols = rights[0].shape[1]
        many = len(plan[0][2])
        size = plan[0][3]
        out = shape_of(
            (count // 2, rows, cols + (more.shape[1] if more is not None else 0)), BF16
        )
        return call(
            functools.partial(
                weight_grad_kernel,
                lefts=len(lefts),
                rights=len(rights),
                plan=tuple(plan),
                rows=rows,
                extra=more is not None,
            ),
            name,
            [out] * (2 * many),
            where=where,
            in_specs=[untouched()] * (len(lefts) + len(rights))
            + ([whole(more)] if more is not None else []),
            out_specs=wholes([out] * (2 * many)),
            scratch=[
                pltpu.VMEM((2, size, width), BF16),
                pltpu.VMEM((2, many, size, cols), BF16),
                pltpu.VMEM((many, width, cols), F32),
                pltpu.SemaphoreType.DMA((1 + many, 2)),
            ],
            flops=2 * sequence * width * cols * many,
            moved=sequence * (width + cols * many) * 2,
        )(*lefts, *rights, *([more] if more is not None else []))

    def with_theirs(left, right):
        grad = dot_rows(left, right).astype(BF16)
        blocks = grad.reshape(count // 2, 2, rows, grad.shape[1])
        return grad, lax.dynamic_index_in_dim(blocks, 1 - where[1] % 2, 1, keepdims=False)

    gate_grad, gate_theirs = with_theirs(second_in, after(grad_gate, back_sum, back_near))
    gate_got = swapped(gate_theirs, "dp", 1)
    down_grad, down_theirs = with_theirs(cotangents, after(hidden_act, gate_grad))
    up_grad, up_theirs = with_theirs(second_in, after(grad_up, down_grad))

    def to_owners(matrices, name):
        cols = matrices[0][0].shape[1]
        parts = [part for parts in matrices for part in parts]
        blocks_out = shape_of((sum(p[0].shape[1] for p in matrices) // cols, owned, cols), BF16)
        blocks = call(
            functools.partial(
                finish_sum_kernel, terms=tuple(len(parts) for parts in matrices), owned=owned
            ),
            name + "_finish",
            [blocks_out] * GROUP,
            where=where,
            in_specs=wholes(parts),
            out_specs=[whole(blocks_out)] * GROUP,
            scratch=[pltpu.VMEM((GROUP, owned, cols), F32)],
            flops=0,
            moved=rows * cols * 2 * (len(parts) + 1),
        )(*parts)
        return [blocks[0]] + [swapped(blocks[k], "group", k) for k in range(1, GROUP)]

    def halved(mine, got, name):
        half = shape_of((mine.shape[0] // 2,) + mine.shape[1:], BF16)
        return call(
            halve_kernel,
            name,
            [half, half],
            where=where,
            in_specs=wholes([mine, got]),
            out_specs=wholes([half, half]),
            flops=0,
            moved=mine.size * 6,
        )(mine, got)

    def first_halved(grad, got, name):
        cols = grad.shape[1]
        half = shape_of((count // 4, rows, cols), BF16)

        def mine(bit):
            return pl.BlockSpec(
                (rows, cols),
                lambda j, w: (2 * ((2 * j + bit) ^ (w[1] // 2)) + w[1] % 2, 0),
            )

        def theirs(bit):
            return pl.BlockSpec(
                (None, rows, cols), lambda j, w: ((2 * j + bit) ^ (w[1] // 2), 0, 0)
            )

        out = pl.BlockSpec((None, rows, cols), lambda j, w: (j, 0, 0))
        return call(
            first_halve_kernel,
            name,
            [half, half],
            where=where,
            grid=(count // 4,),
            in_specs=[mine(0), mine(1), theirs(0), theirs(1)],
            out_specs=[out, out],
            flops=0,
            moved=grad.size * 3,
        )(grad, grad, got, got)

    def z_summed(keep, send, name):
        distance = 2
        got = swapped(send, "dp", distance)
        while keep.shape[0] > 1:
            keep, send = halved(keep, got, name)
            distance *= 2
            got = swapped(send, "dp", distance)
        return [keep.reshape(keep.shape[1:]), got.reshape(got.shape[1:])]

    block_f = shape_of((length, width), F32)
    row_f = shape_of((1, width), F32)
    slice_b = shape_of((length, part), BF16)
    pair_b = shape_of((length, 2 * part), BF16)
    by_tile = lambda s: pl.BlockSpec((tile, s.shape[1]), lambda i, w: (i, 0))
    grad_resid, grad_mixed, gain_two, *mixer_sent = call(
        functools.partial(residual_back_kernel, part=part),
        "residual_back",
        [block_f, block_b, row_f, slice_b, slice_b, pair_b],
        where=where,
        grid=(tiles,),
        in_specs=[by_tile(s) for s in (block_b, block_b, block_b, block_f, block_b)]
        + wholes([small_all, w_out]),
        out_specs=[by_tile(block_f), by_tile(block_b), whole(row_f)]
        + [by_tile(s) for s in (slice_b, slice_b, pair_b)],
        scratch=[pltpu.VMEM((tile, width), BF16)],
        flops=2 * length * width * width,
        moved=length * width * 20,
    )(after(back_0, up_grad, out_near), back_near, back_got, residual, cotangent, small_all, w_out)
    mixer_got_far = swapped(mixer_sent[2], "group", FAR)
    mixer_got_other = swapped(mixer_sent[1], "group", NEAR)
    cols_b = shape_of((width, part), BF16)
    w_out_parts = call(
        functools.partial(out_grad_kernel, part=part),
        "out_grad",
        [cols_b] * GROUP,
        where=where,
        grid=(width // 256,),
        in_specs=[pl.BlockSpec((length, 256), lambda i, w: (0, i)), whole(block_b)],
        out_specs=[pl.BlockSpec((256, part), lambda i, w: (i, 0))] * GROUP,
        scratch=[pltpu.VMEM((256, width), F32)],
        flops=2 * length * width * width,
        moved=length * width * 6,
    )(mixer_own, grad_mixed)
    w_out_sum = for_far(w_out_parts[2], w_out_parts[3])
    down_got = swapped(down_theirs, "dp", 1)
    up_got = swapped(up_theirs, "dp", 1)
    gate_sums = first_halved(after(gate_grad, w_out_parts[0]), gate_got, "gate_pair")
    down_sums = first_halved(after(down_grad, gate_sums[0]), down_got, "down_pair")
    gate_z = z_summed(*gate_sums, "gate_half")
    down_z = z_summed(*down_sums, "down_half")
    mixer_got_near = after(mixer_got_far, w_out_sum, down_sums[0])[:, part:]
    grad_mixer_in = [mixer_sent[0], mixer_got_other, mixer_got_far]
    grad_mixer_in += [swapped(mixer_got_near, "group", NEAR)]
    w_out_got = swapped(w_out_sum, "group", FAR)
    w_out_near = swapped(w_out_parts[1], "group", NEAR)
    w_out_grad = (
        w_out_parts[0].astype(F32) + w_out_near.astype(F32) + w_out_got.astype(F32)
    ).astype(BF16)

    taps_f = shape_of((8, part), F32)
    proj_b = shape_of((sequence, 3 * part), BF16)
    last_first = lambda s: pl.BlockSpec((tile, s.shape[1]), lambda i, w: (steps - 1 - i, 0))
    grad_projected, tap_terms, gain_one, *grad_first = call(
        functools.partial(mixer_back_kernel, tiles=tiles, part=part),
        "mixer_back",
        [proj_b, taps_f, row_f] + [block_b] * GROUP,
        where=where,
        grid=(steps,),
        in_specs=[pl.BlockSpec((tile, part), in_block(k, True)) for k in range(GROUP)]
        + [pl.BlockSpec((tile, width), in_block(k, True)) for k in range(GROUP)]
        + [last_first(projected), last_first(convolved)]
        + wholes([small_all, w_in]),
        out_specs=[last_first(proj_b), whole(taps_f), whole(row_f)]
        + [pl.BlockSpec((tile, width), in_block(k, True)) for k in range(GROUP)],
        scratch=[
            pltpu.VMEM((tile, part), BF16),
            pltpu.VMEM((tile, width), BF16),
            pltpu.VMEM((8, part), F32),
        ],
        flops=2 * sequence * width * 3 * part,
        moved=sequence * width * 10,
    )(
        *grad_mixer_in,
        *tokens_of,
        projected,
        convolved,
        after(small_all, gate_sums[0]),
        w_in,
    )

    mixer_mine, mixer_theirs = weight_grad(
        [first_in],
        [after(grad_projected, gate_sums[0], down_sums[0])],
        [(0, k * length, ((0, k * length),), length) for k in range(GROUP)],
        "in_grad",
        more=w_out_grad,
    )
    mixer_got = swapped(after(mixer_theirs, up_got), "dp", 1)
    hold = (mixer_mine, up_got)
    out_got = swapped(after(out_sum, *hold), "group", FAR)
    first_sum = for_far(grad_first[2], after(grad_first[3], *hold))
    first_got = swapped(first_sum, "group", FAR)
    first_near = swapped(after(grad_first[1], *hold), "group", NEAR)
    up_sums = first_halved(after(up_grad, first_sum, first_near), up_got, "up_pair")
    up_z = z_summed(*up_sums, "up_half")
    mixer_sums = halved(
        after(mixer_mine, up_sums[0], gate_z[1], down_z[1]), mixer_got, "mixer_pair"
    )
    mixer_z = z_summed(*mixer_sums, "mixer_half")
    ffn_grads = to_owners([gate_z, up_z, down_z], "ffn")

    block_out = residual + (out_0.astype(F32) + out_near.astype(F32) + out_got.astype(F32))

    tokens_grad = call(
        tokens_grad_kernel,
        "tokens_grad",
        block_f,
        where=where,
        grid=(tiles,),
        in_specs=[by_tile(s) for s in (block_b, block_b, block_b, block_b, block_f)]
        + [whole(small_all)],
        out_specs=by_tile(block_f),
        flops=0,
        moved=length * width * 16,
    )(grad_first[0], first_near, first_got, tokens, grad_resid, small_all)

    mixer_z[0] = after(mixer_z[0], ffn_grads[0], tokens_grad, block_out)
    mixer_grads = to_owners([mixer_z], "mixer")
    mixer_grads = [grad.reshape(owned, width) for grad in mixer_grads]

    gains = jnp.concatenate([gain_one, gain_two], axis=0).reshape(2, GROUP, part)
    gains = [
        lax.dynamic_index_in_dim(gains, where[0] ^ k, 1, keepdims=False) for k in range(GROUP)
    ]
    near = jnp.concatenate([after(gains[1], mixer_grads[0]), gains[3]], axis=0)
    near = jnp.concatenate([gains[0], gains[2]], axis=0) + swapped(near, "group", NEAR)
    small_grad = jnp.concatenate([near[:2] + swapped(near[2:], "group", FAR), tap_terms[:3]], axis=0)
    distance = 1
    while distance < count:
        small_grad = small_grad + swapped(small_grad, "dp", distance)
        distance *= 2

    states = [mixer_master, mixer_first, mixer_second]
    mixer_f, mixer_s, mixer_n = call(
        functools.partial(mixer_adam_kernel, part=part),
        "mixer_adam",
        [shape_of(mixer_master.shape, F32)] * 3,
        where=where,
        in_specs=wholes(mixer_grads + states),
        out_specs=wholes(states),
        scratch=[pltpu.VMEM(mixer_master.shape, F32)],
        flops=0,
        moved=owned * width * 4 * 26,
    )(*mixer_grads, *states)

    states = [ffn_flat, ffn_first.transpose(1, 0, 2), ffn_second.transpose(1, 0, 2)]
    plane = pl.BlockSpec((1, owned, hidden), lambda i, w: (i, 0, 0))
    ffn_new = call(
        functools.partial(ffn_adam_kernel, part=hpart),
        "ffn_adam",
        [shape_of(ffn_flat.shape, F32)] * 3,
        where=where,
        grid=(3,),
        in_specs=[pl.BlockSpec((None, owned, hpart), lambda i, w: (i, 0, 0))] * GROUP + [plane] * 3,
        out_specs=[plane] * 3,
        scratch=[pltpu.VMEM((owned, hidden), F32)],
        flops=0,
        moved=owned * hidden * 3 * 26,
    )(*ffn_grads, *states)
    ffn_f, ffn_s, ffn_n = [new.transpose(1, 0, 2) for new in ffn_new]

    small_f, small_s, small_n = adamw(
        small_master, small_first, small_second, small_grad, rate_small, 0.0
    )

    return (
        block_out,
        tokens_grad,
        mixer_f,
        mixer_s,
        mixer_n,
        ffn_f,
        ffn_s,
        ffn_n,
        small_f,
        small_s,
        small_n,
    )


def solution(mesh):
    both = ("dp", "group")
    matrix = P(both, None)
    stack = P(both, None, None)
    small = P(None, "group")
    in_specs = (matrix, P("dp"), matrix) + (matrix,) * 3 + (stack,) * 3 + (small,) * 3
    out_specs = (matrix, matrix) + (matrix,) * 3 + (stack,) * 3 + (small,) * 3
    return jax.shard_map(local, mesh=mesh, in_specs=in_specs, out_specs=out_specs, check_vma=False)
```

time: 1560 us -> 509 us (0.33)
  waiting for transfers between devices: 1300 us -> 147 us
  Pallas kernels: 0 us -> 213 us
  matrix products: 160 us -> 30.8 us
  starting transfers between devices: 3.11 us -> 56.2 us
  blocking collectives: 27.1 us -> 0 us
    all_gather x4 -> x1, waiting for transfers between devices: 690 us -> 0.02 us  [local(): lax.all_gather(lax.optimization_barrier((ffn_own_rows[0], mixer_z[0], mix...]
    reduce_scatter x3 -> x0, waiting for transfers between devices: 611 us -> none  [the longest x1 578 us: local(): lax.psum_scatter(weight_terms(jnp.int32(0), owned_rows * group_count * la...]
    pallas_call x0 -> x24, Pallas kernels: none -> 213 us  [call(): run(where, trace.ready(first), *rest)]
    ppermute x2 -> x60, waiting for transfers between devices: 0.52 us -> 147 us  [swapped(): return trace.done(lax.ppermute(trace.ready(block), axis, pairs))]
    dot_general x15 -> x3, matrix products: 160 us -> 30.8 us  [dot_rows(): lax.dot_general(left, right, (((0,), (0,)), ((), ())), preferred_element_...]
    ppermute x2 -> x60, starting transfers between devices: 2.83 us -> 56.2 us  [swapped(): return trace.done(lax.ppermute(trace.ready(block), axis, pairs))]
    psum x1 -> x0, blocking collectives: 21.9 us -> none  [local(): small_grad = lax.psum(small_part, 'dp')]
  transfers between devices with their start and end apart: 9 -> 61, of which waited for: 8 -> 24; matrix products, arithmetic and copies ran while one was open for 4% -> 12% of each run, Pallas kernels for 0% -> 40%
where the time goes in v1:
time: 509 us; the launch traced here: 499 us
  Pallas kernels  213 us (42%)
  waiting for transfers between devices  147 us (29%)
  starting transfers between devices  56.2 us (11%)
  matrix products  30.8 us (6%)
  local copies, waits for them, and re-layouts  18.7 us (4%)
  other arithmetic  18.6 us (4%)
  between operations  15.2 us (3%)
    pallas_call x24, Pallas kernels, call(): run(where, trace.ready(first), *rest)  213 us
    ppermute x60, waiting for transfers between devices, swapped(): return trace.done(lax.ppermute(trace.ready(block), axis, pairs))  147 us
    ppermute x60, starting transfers between devices, swapped(): return trace.done(lax.ppermute(trace.ready(block), axis, pairs))  56.2 us
    dot_general x3, matrix products, dot_rows(): lax.dot_general(left, right, (((0,), (0,)), ((), ())), preferred_element_...  30.8 us
    unnamed x125, local copies, waits for them, and re-layouts  14.1 us
  transfers between devices with their start and end apart: 61, of which 24 were waited for; matrix products, arithmetic and copies ran while one was open for 12% of the time, Pallas kernels for 40%

profile of v1, /device:TPU:0, one launch (start us, length us, event | category | flops | bytes accessed | tf_op | source)
XLA Modules:
  0.0 499.5 jit_solution(17764857397606370010)
XLA Ops:
  7.8 3.5 send.1
  14.4 7.2 %collective-permute-done.3.refs_3_ = bf16[32,4736]{1,0:T(8,128)(2,1)S(1)} collective-permute-done((bf16[32,4736]{1,0:T(8,128)(2,1)}, bf16[32,4736]{1,0:T(8,128)(2,1)S(1)}, u32[]{:S(2)}, u32[]{:S(2)}) %collective-permute-start.3) | collective-permute-done | bytes 303136 | tf_op jit(solution)/shard_map/ppermute | solution.py:74
  21.6 6.5 %collective-permute-done.2.refs_2_ = bf16[32,4736]{1,0:T(8,128)(2,1)S(1)} collective-permute-done((bf16[32,4736]{1,0:T(8,128)(2,1)}, bf16[32,4736]{1,0:T(8,128)(2,1)S(1)}, u32[]{:S(2)}, u32[]{:S(2)}) %collective-permute-start.2) | collective-permute-done | bytes 303136 | tf_op jit(solution)/shard_map/ppermute | solution.py:74
  28.9 3.0 take.1
  31.9 3.4 collective-permute-start.6
  38.4 9.4 %collective-permute-done.6.refs_4_.refs_9_ = bf16[128,1024]{1,0:T(8,128)(2,1)S(1)} collective-permute-done((bf16[128,1024]{1,0:T(8,128)(2,1)}, bf16[128,1024]{1,0:T(8,128)(2,1)S(1)}, u32[]{:S(2)}, u32[]{:S(2)}) %collective-permute-start.6) | collective-permute-done | bytes 262176 | tf_op jit(solution)/shard_map/ppermute | solution.py:74
  49.1 6.3 %collective-permute-done.7.refs_6_.refs_11_ = bf16[128,1024]{1,0:T(8,128)(2,1)S(1)} collective-permute-done((bf16[128,1024]{1,0:T(8,128)(2,1)S(1)}, bf16[128,1024]{1,0:T(8,128)(2,1)S(1)}, u32[]{:S(2)}, u32[]{:S(2)}) %collective-permute-start.7) | collective-permute-done | bytes 262176 | tf_op jit(solution)/shard_map/ppermute | solution.py:74
  60.4 14.7 %collective-permute-done.10.refs_5_.refs_10_ = bf16[128,1024]{1,0:T(8,128)(2,1)S(1)} collective-permute-done((bf16[128,1024]{1,0:T(8,128)(2,1)S(1)}, bf16[128,1024]{1,0:T(8,128)(2,1)S(1)}, u32[]{:S(2)}, u32[]{:S(2)}) %collective-permute-start.10) | collective-permute-done | bytes 262176 | tf_op jit(solution)/shard_map/ppermute | solution.py:74
  75.1 8.2 %collective-permute-done.11.refs_7_.refs_12_ = bf16[128,1024]{1,0:T(8,128)(2,1)S(1)} collective-permute-done((bf16[128,1024]{1,0:T(8,128)(2,1)S(1)}, bf16[128,1024]{1,0:T(8,128)(2,1)S(1)}, u32[]{:S(2)}, u32[]{:S(2)}) %collective-permute-start.11) | collective-permute-done | bytes 262176 | tf_op jit(solution)/shard_map/ppermute | solution.py:74
  83.4 7.1 %collective-permute-done.4.refs_2_.refs_6_ = bf16[768,1024]{1,0:T(8,128)(2,1)} collective-permute-done((bf16[768,1024]{1,0:T(8,128)(2,1)S(1)}, bf16[768,1024]{1,0:T(8,128)(2,1)}, u32[]{:S(2)}, u32[]{:S(2)}) %collective-permute-start.4) | collective-permute-done | bytes 1572896 | tf_op jit(solution)/shard_map/ppermute | solution.py:74
  91.3 2.6 stack.13.refs_9_
  95.2 17.1 %mixer_in.1 = (bf16[3072,1024]{1,0:T(8,128)(2,1)}, f32[3072,768]{1,0:T(8,128)}, f32[3072,256]{1,0:T(8,128)}, bf16[3072,256]{1,0:T(8,128)(2,1)}, bf16[1024,768]{1,0:T(8,128)(2,1)}) custom-call(s32[4]{0:T(128)} %pad_add_fusion.where, bf16[768,1024]{1,0:T(8,128)(2,1)} %tokens.1, bf16[768,1024]{1,0:T(8,128)(2,1)} %collective-permute-done.refs_1_.refs_5_, ...), custom_call_target="tpu_custom_call" | custom-call | flops 4831838 | bytes 25165 | tf_op jit(solution)/shard_map/mixer_in/pallas_call | solution.py:107
  116.0 33.1 %collective-permute-done.15.refs_6_ = bf16[3072,256]{1,0:T(8,128)(2,1)S(1)} collective-permute-done((bf16[3072,256]{1,0:T(8,128)(2,1)}, bf16[3072,256]{1,0:T(8,128)(2,1)S(1)}, u32[]{:S(2)}, u32[]{:S(2)}) %collective-permute-start.15) | collective-permute-done | bytes 1572896 | tf_op jit(solution)/shard_map/ppermute | solution.py:74
  152.7 19.2 %residual.1 = (bf16[3072,1024]{1,0:T(8,128)(2,1)}, f32[768,1024]{1,0:T(8,128)}, bf16[768,1024]{1,0:T(8,128)(2,1)}, bf16[1024,1024]{1,0:T(8,128)(2,1)}) custom-call(s32[4]{0:T(128)} %pad_add_fusion.where, bf16[768,1024]{1,0:T(8,128)(2,1)} %tokens.1, bf16[768,1024]{1,0:T(8,128)(2,1)} %collective-permute-done.refs_1_.refs_5_, ...), custom_call_target="tpu_custom_call" | custom-call | flops 6442450 | bytes 25165 | tf_op jit(solution)/shard_map/residual/pallas_call | solution.py:107
  171.9 35.3 %ffn_own.1 = (bf16[3072,1152]{1,0:T(8,128)(2,1)}, bf16[3072,1152]{1,0:T(8,128)(2,1)}, bf16[3072,1152]{1,0:T(8,128)(2,1)}, bf16[3072,1024]{1,0:T(8,128)(2,1)}, bf...) custom-call(s32[4]{0:T(128)} %pad_add_fusion.where, ...), custom_call_target="tpu_custom_call" | custom-call | flops 21743272 | bytes 30277 | tf_op jit(solution)/shard_map/ffn_own/pallas_call | solution.py:107
  207.8 6.4 %copy.45.refs_6_ = bf16[3072,1152]{1,0:T(8,128)(2,1)} copy(bf16[3072,1152]{1,0:T(8,128)(2,1)} %get-tuple-element.158) | data formatting | bytes 14155776
  215.3 35.7 %ffn_far.1 = (bf16[3072,1152]{1,0:T(8,128)(2,1)}, bf16[3072,1152]{1,0:T(8,128)(2,1)}, bf16[3072,1152]{1,0:T(8,128)(2,1)}, bf16[3072,1024]{1,0:T(8,128)(2,1)}, bf...) custom-call(s32[4]{0:T(128)} %pad_add_fusion.where, ...), custom_call_target="tpu_custom_call", output_to_operand_aliasing={{0}: (7, {}), {1}: (8, {}), {2}: (9, {}), {3}: (10, {})} | custom-call | flops 21743272 | bytes 30277 | tf_op jit(solution)/shard_map/ffn_far/pallas_call | solution.py:107
  251.6 3.9 collective-permute-done.25
  258.6 12.7 %convolution_convert_fusion.2.mine_keep.mine_send = bf16[1024,1152]{1,0:T(8,128)(2,1)S(1)} fusion(bf16[3072,1024]{1,0:T(8,128)(2,1)} %get-tuple-element.153.refs_0_, bf16[3072,1152]{1,0:T(8,128)(2,1)} %get-tuple-element.175), kind=kOutput, calls=%fused_computation.2 | convolution fusion | flops 7248936960 | bytes 15728640 | tf_op jit(solution)/shard_map/dot_general | solution.py:37
  274.0 9.1 %convolution_convert_fusion.1.mine_keep.mine_send = bf16[1024,1152]{1,0:T(8,128)(2,1)S(1)} fusion(bf16[3072,1024]{1,0:T(8,128)(2,1)S(1)} %bitcast.63, bf16[3072,1152]{1,0:T(8,128)(2,1)S(1)} %bitcast.52), kind=kOutput, calls=%fused_computation.1 | convolution fusion | flops 7248936960 | bytes 15728640 | tf_op jit(solution)/shard_map/dot_general | solution.py:37
  285.1 9.0 %convolution_convert_fusion.mine_keep.mine_send = bf16[1024,1152]{1,0:T(8,128)(2,1)S(1)} fusion(bf16[3072,1024]{1,0:T(8,128)(2,1)S(1)} %bitcast.54, bf16[3072,1152]{1,0:T(8,128)(2,1)S(1)} %bitcast.59), kind=kOutput, calls=%fused_computation | convolution fusion | flops 7248936960 | bytes 15728640 | tf_op jit(solution)/shard_map/dot_general | solution.py:37
  294.4 9.5 %residual_back.1 = (f32[768,1024]{1,0:T(8,128)}, bf16[768,1024]{1,0:T(8,128)(2,1)}, f32[1,1024]{1,0:T(1,128)}, bf16[768,256]{1,0:T(8,128)(2,1)}, bf16[768,256]{1,0:T(8,128)(2,1)}, /*index=5*/bf16[768,512]{1,0:T(8,128)(2,1)}) custom-call(s32[4]{0:T(128)} %pad_add_fusion.where, bf16[768,1024]{1,0:T(8,128)(2,1)} %get-tuple-element.178.g0, ...), custom_call_target="tpu_custom_call" | custom-call | flops 1610612 | bytes 15728 | tf_op jit(solution)/shard_map/residual_back/pallas_call | solution.py:107
  305.1 6.2 %out_grad.1 = (bf16[1024,256]{1,0:T(8,128)(2,1)}, bf16[1024,256]{1,0:T(8,128)(2,1)}, bf16[1024,256]{1,0:T(8,128)(2,1)}, bf16[1024,256]{1,0:T(8,128)(2,1)}) custom-call(s32[4]{0:T(128)} %pad_add_fusion.where, bf16[768,1024]{1,0:T(8,128)(2,1)} %get-tuple-element.183.left, bf16[768,1024]{1,0:T(8,128)(2,1)} %get-tuple-element.184.right), custom_call_target="tpu_custom_call" | custom-call | flops 1610612 | bytes 4718 | tf_op jit(solution)/shard_map/out_grad/pallas_call | solution.py:107
  314.5 3.2 gate_pair.1
  317.7 9.2 %collective-permute-done.30.got_keep.got_send = bf16[4,128,1152]{2,1,0:T(8,128)(2,1)S(1)} collective-permute-done((bf16[4,128,1152]{2,1,0:T(8,128)(2,1)}, bf16[4,128,1152]{2,1,0:T(8,128)(2,1)S(1)}, u32[]{:S(2)}, u32[]{:S(2)}) %collective-permute-start.30) | collective-permute-done | bytes 1179680 | tf_op jit(solution)/shard_map/ppermute | solution.py:74
  327.9 3.4 down_pair.1
  335.4 2.5 collective-permute-start.38
  338.0 19.1 %mixer_back.1 = (bf16[3072,768]{1,0:T(8,128)(2,1)}, f32[8,256]{1,0:T(8,128)}, f32[1,1024]{1,0:T(1,128)}, bf16[768,1024]{1,0:T(8,128)(2,1)}, bf16[768,1024]{1,0:T...) custom-call(s32[4]{0:T(128)} %pad_add_fusion.where, bf16[768,256]{1,0:T(8,128)(2,1)} %get-tuple-element.180.refs_0_, ...), custom_call_target="tpu_custom_call" | custom-call | flops 4831838 | bytes 31457 | tf_op jit(solution)/shard_map/mixer_back/pallas_call | solution.py:107
  359.5 13.1 %in_grad.1 = (bf16[4,128,1024]{2,1,0:T(8,128)(2,1)}, bf16[4,128,1024]{2,1,0:T(8,128)(2,1)}) custom-call(s32[4]{0:T(128)} %pad_add_fusion.where, bf16[3072,1024]{1,0:T(8,128)(2,1)} %get-tuple-element.165.refs_0_, bf16[3072,768]{1,0:T(8,128)(2,1)} %get-tuple-element.198.refs_1_, bf16[1024,256]{1,0:T(8,128)(2,1)} %add_convert_fusion.3.refs_2_), custom_call_target="tpu_custom_call" | custom-call | flops 4831838 | bytes 11010 | tf_op jit(solution)/shard_map/in_grad/pallas_call | solution.py:107
  373.3 3.3 add_convert_fusion.2
  378.8 2.8 gate_half.1
  381.6 3.9 collective-permute-start.41
  385.4 3.4 up_pair.1
  390.4 3.2 add_convert_fusion
  395.8 2.8 down_half.1
  398.9 13.6 %collective-permute-done.43 = bf16[1,128,1152]{2,1,0:T(8,128)(2,1)S(1)} collective-permute-done((bf16[1,128,1152]{2,1,0:T(8,128)(2,1)}, bf16[1,128,1152]{2,1,0:T(8,128)(2,1)S(1)}, u32[]{:S(2)}, u32[]{:S(2)}) %collective-permute-start.43) | collective-permute-done | bytes 294944 | tf_op jit(solution)/shard_map/ppermute | solution.py:74
  413.2 3.6 mixer_pair.1
  416.8 5.3 %collective-permute-start.46 = (bf16[2,128,1024]{2,1,0:T(8,128)(2,1)}, bf16[2,128,1024]{2,1,0:T(8,128)(2,1)}, u32[]{:S(2)}, u32[]{:S(2)}) collective-permute-start(bf16[2,128,1024]{2,1,0:T(8,128)(2,1)} %get-tuple-element.228), channel_id=1, source_target_pairs={{0,8},{4,12},{8,0},{12,4},{16,24},{20,28},{24,16},{28,20},{1,9},{5... | collective-permute-start | bytes 1572872 | tf_op jit(solution)/shard_map/ppermute | solution.py:74
  422.2 2.8 up_half.1
  425.3 14.3 %collective-permute-done.46.got = bf16[2,128,1024]{2,1,0:T(8,128)(2,1)} collective-permute-done((bf16[2,128,1024]{2,1,0:T(8,128)(2,1)}, bf16[2,128,1024]{2,1,0:T(8,128)(2,1)}, u32[]{:S(2)}, u32[]{:S(2)}) %collective-permute-start.46) | collective-permute-done | bytes 524320 | tf_op jit(solution)/shard_map/ppermute | solution.py:74
  439.6 2.7 mixer_half.1
  442.3 5.1 %add_add_fusion = f32[768,1024]{1,0:T(8,128)} fusion(f32[768,1024]{1,0:T(8,128)S(1)} %copy-done.5, bf16[768,1024]{1,0:T(8,128)(2,1)} %collective-permute-done.36, bf16[768,1024]{1,0:T(8,128)(2,1)} %collective-permute-done.20, bf16[768,1024]{1,0:T(8,128)(2,1)} %get-tuple-element.156), kind=kLoop, calls=%fused_computation.4 | loop fusion | flops 4718592 | bytes 11010048 | tf_op jit(solution)/shard_map/add | solution.py:964
  448.2 3.3 ffn_finish.1
  451.5 6.7 %tokens_grad.1 = f32[768,1024]{1,0:T(8,128)} custom-call(s32[4]{0:T(128)} %pad_add_fusion.where, bf16[768,1024]{1,0:T(8,128)(2,1)} %get-tuple-element.206.g0, bf16[768,1024]{1,0:T(8,128)(2,1)} %copy-done.11, bf16[768,1024]{1,0:T(8,128)(2,1)} %collective-permute-done.40.g2, bf16[768,1024]{1,0:T(8,128)(2,1)} %tokens.1, ...), custom_call_target="tpu_custom_call" | custom-call | bytes 12582 | tf_op jit(solution)/shard_map/tokens_grad/pallas_call | solution.py:107
  463.4 2.9 collective-permute-done.53
  474.1 2.6 collective-permute-start.59
  479.6 7.5 %ffn_adam.1 = (f32[3,32,4608]{2,1,0:T(8,128)}, f32[3,32,4608]{2,1,0:T(8,128)}, f32[3,32,4608]{2,1,0:T(8,128)}) custom-call(s32[4]{0:T(128)} %pad_add_fusion.where, bf16[3,32,1152]{2,1,0:T(8,128)(2,1)} %get-tuple-element.251.g0, bf16[3,32,1152]{2,1,0:T(8,128)(2,1)} %copy-done.37, bf16[3,32,1152]{2,1,0:T(8,128)(2,1)} %copy-done.36, ...), custom_call_target="tpu_custom_call" | custom-call | bytes 11501 | tf_op jit(solution)/shard_map/ffn_adam/pallas_call | solution.py:107
  488.4 3.8 mixer_adam.1
  (256 shorter events, 71.0 us)
Async XLA Ops:
  7.2 164.7 %all-gather.2.cloned.1.call-start = ((), (), s32[]{:S(2)}) async-start(), calls=%async_computation | async-start | bytes 7962624 | tf_op jit(solution)/shard_map/all_gather | solution.py:594
  11.3 10.3 %collective-permute-start.3 = (bf16[32,4736]{1,0:T(8,128)(2,1)}, bf16[32,4736]{1,0:T(8,128)(2,1)S(1)}, u32[]{:S(2)}, u32[]{:S(2)}) collective-permute-start(bf16[32,4736]{1,0:T(8,128)(2,1)} %get-tuple-element.137), channel_id=1, source_target_pairs={{0,3},{1,2},{2,1},{3,0},{4,7},{5,6},{6,5},{7,4},{8,11},{9,10},{10,... | collective-permute-start | bytes 909320 | tf_op jit(solution)/shard_map/ppermute | solution.py:74
  14.4 13.8 %collective-permute-start.2 = (bf16[32,4736]{1,0:T(8,128)(2,1)}, bf16[32,4736]{1,0:T(8,128)(2,1)S(1)}, u32[]{:S(2)}, u32[]{:S(2)}) collective-permute-start(bf16[32,4736]{1,0:T(8,128)(2,1)} %get-tuple-element.136), channel_id=1, source_target_pairs={{0,2},{1,3},{2,0},{3,1},{4,6},{5,7},{6,4},{7,5},{8,10},{9,11},{10,... | collective-permute-start | bytes 909320 | tf_op jit(solution)/shard_map/ppermute | solution.py:74
  31.9 15.8 %collective-permute-start.6 = (bf16[128,1024]{1,0:T(8,128)(2,1)}, bf16[128,1024]{1,0:T(8,128)(2,1)S(1)}, u32[]{:S(2)}, u32[]{:S(2)}) collective-permute-start(bf16[128,1024]{1,0:T(8,128)(2,1)} %bitcast.66), channel_id=1, source_target_pairs={{0,16},{4,20},{8,24},{12,28},{16,0},{20,4},{24,8},{28,12},{1,17},{... | collective-permute-start | bytes 786440 | tf_op jit(solution)/shard_map/ppermute | solution.py:74
  35.3 13.2 %collective-permute-start.8 = (bf16[128,1024]{1,0:T(8,128)(2,1)}, bf16[128,1024]{1,0:T(8,128)(2,1)S(1)}, u32[]{:S(2)}, u32[]{:S(2)}) collective-permute-start(bf16[128,1024]{1,0:T(8,128)(2,1)} %bitcast.67), channel_id=1, source_target_pairs={{0,4},{4,0},{8,12},{12,8},{16,20},{20,16},{24,28},{28,24},{1,5},{5... | collective-permute-start | bytes 786440 | tf_op jit(solution)/shard_map/ppermute | solution.py:74
  36.8 12.3 %collective-permute-start.5 = (bf16[128,1024]{1,0:T(8,128)(2,1)}, bf16[128,1024]{1,0:T(8,128)(2,1)S(1)}, u32[]{:S(2)}, u32[]{:S(2)}) collective-permute-start(bf16[128,1024]{1,0:T(8,128)(2,1)} %bitcast.68), channel_id=1, source_target_pairs={{0,8},{4,12},{8,0},{12,4},{16,24},{20,28},{24,16},{28,20},{1,9},{5... | collective-permute-start | bytes 786440 | tf_op jit(solution)/shard_map/ppermute | solution.py:74
  55.5 35.0 %collective-permute-start.4 = (bf16[768,1024]{1,0:T(8,128)(2,1)S(1)}, bf16[768,1024]{1,0:T(8,128)(2,1)}, u32[]{:S(2)}, u32[]{:S(2)}) collective-permute-start(bf16[768,1024]{1,0:T(8,128)(2,1)S(1)} %copy-done), channel_id=1, source_target_pairs={{0,2},{1,3},{2,0},{3,1},{4,6},{5,7},{6,4},{7,5},{8,10},{9,11},{10,... | collective-permute-start | bytes 4718600 | tf_op jit(solution)/shard_map/ppermute | solution.py:74
  56.9 18.2 %collective-permute-start.9 = (bf16[128,1024]{1,0:T(8,128)(2,1)S(1)}, bf16[128,1024]{1,0:T(8,128)(2,1)S(1)}, u32[]{:S(2)}, u32[]{:S(2)}) collective-permute-start(bf16[128,1024]{1,0:T(8,128)(2,1)S(1)} %collective-permute-done.5.refs_2_.refs_7_), channel_id=1, source_target_pairs={{0,4},{4,0},{8,12},{12,8},{16,20},{20,16},{24,28},{28,24},{1,5},{5... | collective-permute-start | bytes 786440 | tf_op jit(solution)/shard_map/ppermute | solution.py:74
  58.4 16.7 %collective-permute-start.10 = (bf16[128,1024]{1,0:T(8,128)(2,1)S(1)}, bf16[128,1024]{1,0:T(8,128)(2,1)S(1)}, u32[]{:S(2)}, u32[]{:S(2)}) collective-permute-start(bf16[128,1024]{1,0:T(8,128)(2,1)S(1)} %collective-permute-done.6.refs_4_.refs_9_), channel_id=1, source_target_pairs={{0,4},{4,0},{8,12},{12,8},{16,20},{20,16},{24,28},{28,24},{1,5},{5... | collective-permute-start | bytes 786440 | tf_op jit(solution)/shard_map/ppermute | solution.py:74
  58.9 24.4 %collective-permute-start.11 = (bf16[128,1024]{1,0:T(8,128)(2,1)S(1)}, bf16[128,1024]{1,0:T(8,128)(2,1)S(1)}, u32[]{:S(2)}, u32[]{:S(2)}) collective-permute-start(bf16[128,1024]{1,0:T(8,128)(2,1)S(1)} %collective-permute-done.7.refs_6_.refs_11_), channel_id=1, source_target_pairs={{0,4},{4,0},{8,12},{12,8},{16,20},{20,16},{24,28},{28,24},{1,5},{5... | collective-permute-start | bytes 786440 | tf_op jit(solution)/shard_map/ppermute | solution.py:74
  60.4 34.7 %collective-permute-start = (bf16[768,1024]{1,0:T(8,128)(2,1)S(1)}, bf16[768,1024]{1,0:T(8,128)(2,1)}, u32[]{:S(2)}, u32[]{:S(2)}) collective-permute-start(bf16[768,1024]{1,0:T(8,128)(2,1)S(1)} %copy-done), channel_id=1, source_target_pairs={{0,1},{1,0},{2,3},{3,2},{4,5},{5,4},{6,7},{7,6},{8,9},{9,8},{10,11... | collective-permute-start | bytes 4718600 | tf_op jit(solution)/shard_map/ppermute | solution.py:74
  93.9 18.3 %collective-permute-start.13 = (bf16[1024,256]{1,0:T(8,128)(2,1)}, bf16[1024,256]{1,0:T(8,128)(2,1)}, u32[]{:S(2)}, u32[]{:S(2)}) collective-permute-start(bf16[1024,256]{1,0:T(8,128)(2,1)} %stack.13.refs_9_), channel_id=1, source_target_pairs={{0,2},{1,3},{2,0},{3,1},{4,6},{5,7},{6,4},{7,5},{8,10},{9,11},{10,... | collective-permute-start | bytes 1572872 | tf_op jit(solution)/shard_map/ppermute | solution.py:74
  112.3 36.9 %collective-permute-start.15 = (bf16[3072,256]{1,0:T(8,128)(2,1)}, bf16[3072,256]{1,0:T(8,128)(2,1)S(1)}, u32[]{:S(2)}, u32[]{:S(2)}) collective-permute-start(bf16[3072,256]{1,0:T(8,128)(2,1)} %get-tuple-element.150.refs_4_), channel_id=1, source_target_pairs={{0,2},{1,3},{2,0},{3,1},{4,6},{5,7},{6,4},{7,5},{8,10},{9,11},{10,... | collective-permute-start | bytes 4718600 | tf_op jit(solution)/shard_map/ppermute | solution.py:74
  113.6 36.8 %collective-permute-start.14 = (bf16[3072,256]{1,0:T(8,128)(2,1)}, bf16[3072,256]{1,0:T(8,128)(2,1)S(1)}, u32[]{:S(2)}, u32[]{:S(2)}) collective-permute-start(bf16[3072,256]{1,0:T(8,128)(2,1)} %get-tuple-element.150.refs_4_), channel_id=1, source_target_pairs={{0,1},{1,0},{2,3},{3,2},{4,5},{5,4},{6,7},{7,6},{8,9},{9,8},{10,11... | collective-permute-start | bytes 4718600 | tf_op jit(solution)/shard_map/ppermute | solution.py:74
  149.1 22.7 %collective-permute-start.19 = (bf16[768,1024]{1,0:T(8,128)(2,1)S(1)}, bf16[768,1024]{1,0:T(8,128)(2,1)}, u32[]{:S(2)}, u32[]{:S(2)}) collective-permute-start(bf16[768,1024]{1,0:T(8,128)(2,1)S(1)} %copy-done.4), channel_id=1, source_target_pairs={{0,1},{1,0},{2,3},{3,2},{4,5},{5,4},{6,7},{7,6},{8,9},{9,8},{10,11... | collective-permute-start | bytes 4718600 | tf_op jit(solution)/shard_map/ppermute | solution.py:74
  149.7 57.5 %collective-permute-start.21 = (bf16[768,1024]{1,0:T(8,128)(2,1)S(1)}, bf16[768,1024]{1,0:T(8,128)(2,1)S(1)}, u32[]{:S(2)}, u32[]{:S(2)}) collective-permute-start(bf16[768,1024]{1,0:T(8,128)(2,1)S(1)} %copy-done.4), channel_id=1, source_target_pairs={{0,2},{1,3},{2,0},{3,1},{4,6},{5,7},{6,4},{7,5},{8,10},{9,11},{10,... | collective-permute-start | bytes 4718600 | tf_op jit(solution)/shard_map/ppermute | solution.py:74
  207.4 43.7 %collective-permute-start.24 = (bf16[768,1024]{1,0:T(8,128)(2,1)}, bf16[768,1024]{1,0:T(8,128)(2,1)}, u32[]{:S(2)}, u32[]{:S(2)}) collective-permute-start(bf16[768,1024]{1,0:T(8,128)(2,1)} %get-tuple-element.173), channel_id=1, source_target_pairs={{0,1},{1,0},{2,3},{3,2},{4,5},{5,4},{6,7},{7,6},{8,9},{9,8},{10,11... | collective-permute-start | bytes 4718600 | tf_op jit(solution)/shard_map/ppermute | solution.py:74
  251.3 42.8 %collective-permute-start.20 = (bf16[768,1024]{1,0:T(8,128)(2,1)}, bf16[768,1024]{1,0:T(8,128)(2,1)}, u32[]{:S(2)}, u32[]{:S(2)}) collective-permute-start(bf16[768,1024]{1,0:T(8,128)(2,1)} %get-tuple-element.157), channel_id=1, source_target_pairs={{0,1},{1,0},{2,3},{3,2},{4,5},{5,4},{6,7},{7,6},{8,9},{9,8},{10,11... | collective-permute-start | bytes 4718600 | tf_op jit(solution)/shard_map/ppermute | solution.py:74
  257.8 36.6 %collective-permute-start.26 = (bf16[768,1024]{1,0:T(8,128)(2,1)S(1)}, bf16[768,1024]{1,0:T(8,128)(2,1)}, u32[]{:S(2)}, u32[]{:S(2)}) collective-permute-start(bf16[768,1024]{1,0:T(8,128)(2,1)S(1)} %add_convert_fusion.1), channel_id=1, source_target_pairs={{0,2},{1,3},{2,0},{3,1},{4,6},{5,7},{6,4},{7,5},{8,10},{9,11},{10,... | collective-permute-start | bytes 4718600 | tf_op jit(solution)/shard_map/ppermute | solution.py:74
  272.6 40.4 %collective-permute-start.29 = (bf16[4,128,1152]{2,1,0:T(8,128)(2,1)}, bf16[4,128,1152]{2,1,0:T(8,128)(2,1)}, u32[]{:S(2)}, u32[]{:S(2)}) collective-permute-start(bf16[4,128,1152]{2,1,0:T(8,128)(2,1)} %dynamic-slice_bitcast_fusion.2), channel_id=1, source_target_pairs={{0,4},{4,0},{8,12},{12,8},{16,20},{20,16},{24,28},{28,24},{1,5},{5... | collective-permute-start | bytes 3538952 | tf_op jit(solution)/shard_map/ppermute | solution.py:74
  284.4 42.5 %collective-permute-start.30 = (bf16[4,128,1152]{2,1,0:T(8,128)(2,1)}, bf16[4,128,1152]{2,1,0:T(8,128)(2,1)S(1)}, u32[]{:S(2)}, u32[]{:S(2)}) collective-permute-start(bf16[4,128,1152]{2,1,0:T(8,128)(2,1)} %dynamic-slice_bitcast_fusion.1), channel_id=1, source_target_pairs={{0,4},{4,0},{8,12},{12,8},{16,20},{20,16},{24,28},{28,24},{1,5},{5... | collective-permute-start | bytes 3538952 | tf_op jit(solution)/shard_map/ppermute | solution.py:74
  303.9 27.4 %collective-permute-start.28 = (bf16[768,512]{1,0:T(8,128)(2,1)}, bf16[768,512]{1,0:T(8,128)(2,1)}, u32[]{:S(2)}, u32[]{:S(2)}) collective-permute-start(bf16[768,512]{1,0:T(8,128)(2,1)} %get-tuple-element.182), channel_id=1, source_target_pairs={{0,2},{1,3},{2,0},{3,1},{4,6},{5,7},{6,4},{7,5},{8,10},{9,11},{10,... | collective-permute-start | bytes 2359304 | tf_op jit(solution)/shard_map/ppermute | solution.py:74
  305.1 21.8 %collective-permute-start.27 = (bf16[768,256]{1,0:T(8,128)(2,1)}, bf16[768,256]{1,0:T(8,128)(2,1)}, u32[]{:S(2)}, u32[]{:S(2)}) collective-permute-start(bf16[768,256]{1,0:T(8,128)(2,1)} %get-tuple-element.181), channel_id=1, source_target_pairs={{0,1},{1,0},{2,3},{3,2},{4,5},{5,4},{6,7},{7,6},{8,9},{9,8},{10,11... | collective-permute-start | bytes 1179656 | tf_op jit(solution)/shard_map/ppermute | solution.py:74
  311.3 21.6 %collective-permute-start.33 = (bf16[1024,256]{1,0:T(8,128)(2,1)}, bf16[1024,256]{1,0:T(8,128)(2,1)S(1)}, u32[]{:S(2)}, u32[]{:S(2)}) collective-permute-start(bf16[1024,256]{1,0:T(8,128)(2,1)} %get-tuple-element.201), channel_id=1, source_target_pairs={{0,1},{1,0},{2,3},{3,2},{4,5},{5,4},{6,7},{7,6},{8,9},{9,8},{10,11... | collective-permute-start | bytes 1572872 | tf_op jit(solution)/shard_map/ppermute | solution.py:74
  313.0 44.1 %collective-permute-start.35 = (bf16[4,128,1152]{2,1,0:T(8,128)(2,1)}, bf16[4,128,1152]{2,1,0:T(8,128)(2,1)S(1)}, u32[]{:S(2)}, u32[]{:S(2)}) collective-permute-start(bf16[4,128,1152]{2,1,0:T(8,128)(2,1)} %dynamic-slice_bitcast_fusion), channel_id=1, source_target_pairs={{0,4},{4,0},{8,12},{12,8},{16,20},{20,16},{24,28},{28,24},{1,5},{5... | collective-permute-start | bytes 3538952 | tf_op jit(solution)/shard_map/ppermute | solution.py:74
  332.4 24.7 %collective-permute-start.32 = (bf16[1024,256]{1,0:T(8,128)(2,1)}, bf16[1024,256]{1,0:T(8,128)(2,1)S(1)}, u32[]{:S(2)}, u32[]{:S(2)}) collective-permute-start(bf16[1024,256]{1,0:T(8,128)(2,1)} %get-tuple-element.199), channel_id=1, source_target_pairs={{0,1},{1,0},{2,3},{3,2},{4,5},{5,4},{6,7},{7,6},{8,9},{9,8},{10,11... | collective-permute-start | bytes 1572872 | tf_op jit(solution)/shard_map/ppermute | solution.py:74
  334.1 23.0 %collective-permute-start.34 = (bf16[1024,256]{1,0:T(8,128)(2,1)S(1)}, bf16[1024,256]{1,0:T(8,128)(2,1)}, u32[]{:S(2)}, u32[]{:S(2)}) collective-permute-start(bf16[1024,256]{1,0:T(8,128)(2,1)S(1)} %add_convert_fusion.4), channel_id=1, source_target_pairs={{0,2},{1,3},{2,0},{3,1},{4,6},{5,7},{6,4},{7,5},{8,10},{9,11},{10,... | collective-permute-start | bytes 1572872 | tf_op jit(solution)/shard_map/ppermute | solution.py:74
  335.4 37.8 %collective-permute-start.38 = (bf16[2,128,1152]{2,1,0:T(8,128)(2,1)}, bf16[2,128,1152]{2,1,0:T(8,128)(2,1)S(1)}, u32[]{:S(2)}, u32[]{:S(2)}) collective-permute-start(bf16[2,128,1152]{2,1,0:T(8,128)(2,1)} %get-tuple-element.212), channel_id=1, source_target_pairs={{0,8},{4,12},{8,0},{12,4},{16,24},{20,28},{24,16},{28,20},{1,9},{5... | collective-permute-start | bytes 1769480 | tf_op jit(solution)/shard_map/ppermute | solution.py:74
  338.0 35.4 %collective-permute-start.23 = (bf16[768,1024]{1,0:T(8,128)(2,1)}, bf16[768,1024]{1,0:T(8,128)(2,1)}, u32[]{:S(2)}, u32[]{:S(2)}) collective-permute-start(bf16[768,1024]{1,0:T(8,128)(2,1)} %get-tuple-element.164), channel_id=1, source_target_pairs={{0,1},{1,0},{2,3},{3,2},{4,5},{5,4},{6,7},{7,6},{8,9},{9,8},{10,11... | collective-permute-start | bytes 4718600 | tf_op jit(solution)/shard_map/ppermute | solution.py:74
  372.7 8.9 %collective-permute-start.37 = (bf16[768,1024]{1,0:T(8,128)(2,1)}, bf16[768,1024]{1,0:T(8,128)(2,1)S(1)}, u32[]{:S(2)}, u32[]{:S(2)}) collective-permute-start(bf16[768,1024]{1,0:T(8,128)(2,1)} %get-tuple-element.208), channel_id=1, source_target_pairs={{0,1},{1,0},{2,3},{3,2},{4,5},{5,4},{6,7},{7,6},{8,9},{9,8},{10,11... | collective-permute-start | bytes 4718600 | tf_op jit(solution)/shard_map/ppermute | solution.py:74
  373.2 15.7 %collective-permute-start.39 = (bf16[768,1024]{1,0:T(8,128)(2,1)}, bf16[768,1024]{1,0:T(8,128)(2,1)}, u32[]{:S(2)}, u32[]{:S(2)}) collective-permute-start(bf16[768,1024]{1,0:T(8,128)(2,1)} %get-tuple-element.213), channel_id=1, source_target_pairs={{0,1},{1,0},{2,3},{3,2},{4,5},{5,4},{6,7},{7,6},{8,9},{9,8},{10,11... | collective-permute-start | bytes 4718600 | tf_op jit(solution)/shard_map/ppermute | solution.py:74
  373.3 22.3 %collective-permute-start.42 = (bf16[2,128,1152]{2,1,0:T(8,128)(2,1)}, bf16[2,128,1152]{2,1,0:T(8,128)(2,1)}, u32[]{:S(2)}, u32[]{:S(2)}) collective-permute-start(bf16[2,128,1152]{2,1,0:T(8,128)(2,1)} %get-tuple-element.219), channel_id=1, source_target_pairs={{0,8},{4,12},{8,0},{12,4},{16,24},{20,28},{24,16},{28,20},{1,9},{5... | collective-permute-start | bytes 1769480 | tf_op jit(solution)/shard_map/ppermute | solution.py:74
  376.7 45.5 %collective-permute-start.36 = (bf16[768,1024]{1,0:T(8,128)(2,1)}, bf16[768,1024]{1,0:T(8,128)(2,1)}, u32[]{:S(2)}, u32[]{:S(2)}) collective-permute-start(bf16[768,1024]{1,0:T(8,128)(2,1)} %add_convert_fusion.2), channel_id=1, source_target_pairs={{0,2},{1,3},{2,0},{3,1},{4,6},{5,7},{6,4},{7,5},{8,10},{9,11},{10,... | collective-permute-start | bytes 4718600 | tf_op jit(solution)/shard_map/ppermute | solution.py:74
  377.4 35.8 %collective-permute-start.44 = (bf16[4,128,1024]{2,1,0:T(8,128)(2,1)}, bf16[4,128,1024]{2,1,0:T(8,128)(2,1)}, u32[]{:S(2)}, u32[]{:S(2)}) collective-permute-start(bf16[4,128,1024]{2,1,0:T(8,128)(2,1)} %get-tuple-element.223), channel_id=1, source_target_pairs={{0,4},{4,0},{8,12},{12,8},{16,20},{20,16},{24,28},{28,24},{1,5},{5... | collective-permute-start | bytes 3145736 | tf_op jit(solution)/shard_map/ppermute | solution.py:74
  381.6 17.3 %collective-permute-start.41 = (bf16[1,128,1152]{2,1,0:T(8,128)(2,1)}, bf16[1,128,1152]{2,1,0:T(8,128)(2,1)S(1)}, u32[]{:S(2)}, u32[]{:S(2)}) collective-permute-start(bf16[1,128,1152]{2,1,0:T(8,128)(2,1)} %get-tuple-element.218), channel_id=1, source_target_pairs={{0,16},{4,20},{8,24},{12,28},{16,0},{20,4},{24,8},{28,12},{1,17},{... | collective-permute-start | bytes 884744 | tf_op jit(solution)/shard_map/ppermute | solution.py:74
  388.9 27.9 %collective-permute-start.45 = (bf16[2,128,1152]{2,1,0:T(8,128)(2,1)}, bf16[2,128,1152]{2,1,0:T(8,128)(2,1)}, u32[]{:S(2)}, u32[]{:S(2)}) collective-permute-start(bf16[2,128,1152]{2,1,0:T(8,128)(2,1)} %get-tuple-element.227), channel_id=1, source_target_pairs={{0,8},{4,12},{8,0},{12,4},{16,24},{20,28},{24,16},{28,20},{1,9},{5... | collective-permute-start | bytes 1769480 | tf_op jit(solution)/shard_map/ppermute | solution.py:74
  395.6 55.9 %collective-permute-start.40 = (bf16[768,1024]{1,0:T(8,128)(2,1)}, bf16[768,1024]{1,0:T(8,128)(2,1)}, u32[]{:S(2)}, u32[]{:S(2)}) collective-permute-start(bf16[768,1024]{1,0:T(8,128)(2,1)} %add_convert_fusion), channel_id=1, source_target_pairs={{0,2},{1,3},{2,0},{3,1},{4,6},{5,7},{6,4},{7,5},{8,10},{9,11},{10,... | collective-permute-start | bytes 4718600 | tf_op jit(solution)/shard_map/ppermute | solution.py:74
  398.9 13.6 %collective-permute-start.43 = (bf16[1,128,1152]{2,1,0:T(8,128)(2,1)}, bf16[1,128,1152]{2,1,0:T(8,128)(2,1)S(1)}, u32[]{:S(2)}, u32[]{:S(2)}) collective-permute-start(bf16[1,128,1152]{2,1,0:T(8,128)(2,1)} %get-tuple-element.220), channel_id=1, source_target_pairs={{0,16},{4,20},{8,24},{12,28},{16,0},{20,4},{24,8},{28,12},{1,17},{... | collective-permute-start | bytes 884744 | tf_op jit(solution)/shard_map/ppermute | solution.py:74
  416.8 22.8 %collective-permute-start.46 = (bf16[2,128,1024]{2,1,0:T(8,128)(2,1)}, bf16[2,128,1024]{2,1,0:T(8,128)(2,1)}, u32[]{:S(2)}, u32[]{:S(2)}) collective-permute-start(bf16[2,128,1024]{2,1,0:T(8,128)(2,1)} %get-tuple-element.228), channel_id=1, source_target_pairs={{0,8},{4,12},{8,0},{12,4},{16,24},{20,28},{24,16},{28,20},{1,9},{5... | collective-permute-start | bytes 1572872 | tf_op jit(solution)/shard_map/ppermute | solution.py:74
  425.0 22.5 %collective-permute-start.47 = (bf16[1,128,1152]{2,1,0:T(8,128)(2,1)}, bf16[1,128,1152]{2,1,0:T(8,128)(2,1)S(1)}, u32[]{:S(2)}, u32[]{:S(2)}) collective-permute-start(bf16[1,128,1152]{2,1,0:T(8,128)(2,1)} %get-tuple-element.233), channel_id=1, source_target_pairs={{0,16},{4,20},{8,24},{12,28},{16,0},{20,4},{24,8},{28,12},{1,17},{... | collective-permute-start | bytes 884744 | tf_op jit(solution)/shard_map/ppermute | solution.py:74
  442.3 15.9 %collective-permute-start.48 = (bf16[1,128,1024]{2,1,0:T(8,128)(2,1)}, bf16[1,128,1024]{2,1,0:T(8,128)(2,1)S(1)}, u32[]{:S(2)}, u32[]{:S(2)}) collective-permute-start(bf16[1,128,1024]{2,1,0:T(8,128)(2,1)} %get-tuple-element.237), channel_id=1, source_target_pairs={{0,16},{4,20},{8,24},{12,28},{16,0},{20,4},{24,8},{28,12},{1,17},{... | collective-permute-start | bytes 786440 | tf_op jit(solution)/shard_map/ppermute | solution.py:74
  467.8 9.7 %collective-permute-start.56 = (bf16[3,32,1152]{2,1,0:T(8,128)(2,1)S(1)}, bf16[3,32,1152]{2,1,0:T(8,128)(2,1)S(1)}, u32[]{:S(2)}, u32[]{:S(2)}) collective-permute-start(bf16[3,32,1152]{2,1,0:T(8,128)(2,1)S(1)} %copy-done.52), channel_id=1, source_target_pairs={{0,2},{1,3},{2,0},{3,1},{4,6},{5,7},{6,4},{7,5},{8,10},{9,11},{10,... | collective-permute-start | bytes 663560 | tf_op jit(solution)/shard_map/ppermute | solution.py:74
  468.5 9.0 %collective-permute-start.55 = (bf16[3,32,1152]{2,1,0:T(8,128)(2,1)S(1)}, bf16[3,32,1152]{2,1,0:T(8,128)(2,1)S(1)}, u32[]{:S(2)}, u32[]{:S(2)}) collective-permute-start(bf16[3,32,1152]{2,1,0:T(8,128)(2,1)S(1)} %copy-done.51), channel_id=1, source_target_pairs={{0,1},{1,0},{2,3},{3,2},{4,5},{5,4},{6,7},{7,6},{8,9},{9,8},{10,11... | collective-permute-start | bytes 663560 | tf_op jit(solution)/shard_map/ppermute | solution.py:74
  468.5 10.4 %collective-permute-start.57 = (bf16[3,32,1152]{2,1,0:T(8,128)(2,1)S(1)}, bf16[3,32,1152]{2,1,0:T(8,128)(2,1)S(1)}, u32[]{:S(2)}, u32[]{:S(2)}) collective-permute-start(bf16[3,32,1152]{2,1,0:T(8,128)(2,1)S(1)} %copy-done.50), channel_id=1, source_target_pairs={{0,3},{1,2},{2,1},{3,0},{4,7},{5,6},{6,5},{7,4},{8,11},{9,10},{10,... | collective-permute-start | bytes 663560 | tf_op jit(solution)/shard_map/ppermute | solution.py:74
  474.1 13.0 %collective-permute-start.59 = (f32[5,256]{1,0:T(8,128)S(1)}, f32[5,256]{1,0:T(8,128)S(1)}, u32[]{:S(2)}, u32[]{:S(2)}) collective-permute-start(f32[5,256]{1,0:T(8,128)S(1)} %add.101), channel_id=1, source_target_pairs={{0,16},{4,20},{8,24},{12,28},{16,0},{20,4},{24,8},{28,12},{1,17},{... | collective-permute-start | bytes 15368 | tf_op jit(solution)/shard_map/ppermute | solution.py:74
  476.7 11.0 %collective-permute-start.50 = (bf16[1,32,1024]{2,1,0:T(8,128)(2,1)}, bf16[1,32,1024]{2,1,0:T(8,128)(2,1)S(1)}, u32[]{:S(2)}, u32[]{:S(2)}) collective-permute-start(bf16[1,32,1024]{2,1,0:T(8,128)(2,1)} %get-tuple-element.242), channel_id=1, source_target_pairs={{0,2},{1,3},{2,0},{3,1},{4,6},{5,7},{6,4},{7,5},{8,10},{9,11},{10,... | collective-permute-start | bytes 196616 | tf_op jit(solution)/shard_map/ppermute | solution.py:74
  477.4 10.3 %collective-permute-start.49 = (bf16[1,32,1024]{2,1,0:T(8,128)(2,1)}, bf16[1,32,1024]{2,1,0:T(8,128)(2,1)S(1)}, u32[]{:S(2)}, u32[]{:S(2)}) collective-permute-start(bf16[1,32,1024]{2,1,0:T(8,128)(2,1)} %get-tuple-element.240), channel_id=1, source_target_pairs={{0,1},{1,0},{2,3},{3,2},{4,5},{5,4},{6,7},{7,6},{8,9},{9,8},{10,11... | collective-permute-start | bytes 196616 | tf_op jit(solution)/shard_map/ppermute | solution.py:74
  477.4 10.3 %collective-permute-start.51 = (bf16[1,32,1024]{2,1,0:T(8,128)(2,1)}, bf16[1,32,1024]{2,1,0:T(8,128)(2,1)S(1)}, u32[]{:S(2)}, u32[]{:S(2)}) collective-permute-start(bf16[1,32,1024]{2,1,0:T(8,128)(2,1)} %get-tuple-element.243), channel_id=1, source_target_pairs={{0,3},{1,2},{2,1},{3,0},{4,7},{5,6},{6,5},{7,4},{8,11},{9,10},{10,... | collective-permute-start | bytes 196616 | tf_op jit(solution)/shard_map/ppermute | solution.py:74
  (74 other events, 1086.3 us)
Sparse Core Ops, SparseCore 0:
  55.6 112.3 all-gather.1

commit v2 on v1

--- a/solution.py
+++ b/solution.py
@@ -65,7 +65,7 @@
         return lax.optimization_barrier([operand] + earlier)[0] if earlier else operand
 
     def done(self, results):
-        self.results.append(jax.tree.leaves(results)[0])
+        self.results.append(jax.tree.leaves(results)[-1])
         return results
 
 
@@ -733,7 +733,7 @@
     )
     cotangent_far = [
         cotangent_far,
-        swapped(lax.optimization_barrier((cotangent_far, kept[0]))[0], "group", NEAR),
+        swapped(lax.optimization_barrier((cotangent_far, out_0))[0], "group", NEAR),
     ]
     hidden_act, grad_gate, grad_up, cotangents, out_2, out_3, back_2, back_3 = ffn_call(
         second_in,

time: 509 us -> 506 us (level)
  local copies, waits for them, and re-layouts: 18.7 us -> 12.3 us
    unnamed x125 -> x124, local copies, waits for them, and re-layouts: 14.1 us -> 7.66 us
  transfers between devices with their start and end apart: 61 -> 61, of which waited for: 24 -> 25; matrix products, arithmetic and copies ran while one was open for 12% -> 11% of each run, Pallas kernels for 40% -> 40%
where the time goes in v2:
time: 506 us; the launch traced here: 497 us
  Pallas kernels  213 us (42%)
  waiting for transfers between devices  151 us (30%)
  starting transfers between devices  56.3 us (11%)
  matrix products  30.8 us (6%)
  other arithmetic  18.6 us (4%)
  between operations  15.2 us (3%)
  local copies, waits for them, and re-layouts  12.3 us (2%)
    pallas_call x24, Pallas kernels, call(): run(where, trace.ready(first), *rest)  213 us
    ppermute x60, waiting for transfers between devices, swapped(): return trace.done(lax.ppermute(trace.ready(block), axis, pairs))  151 us
    ppermute x60, starting transfers between devices, swapped(): return trace.done(lax.ppermute(trace.ready(block), axis, pairs))  56.2 us
    dot_general x3, matrix products, dot_rows(): lax.dot_general(left, right, (((0,), (0,)), ((), ())), preferred_element_...  30.8 us
  transfers between devices with their start and end apart: 61, of which 25 were waited for; matrix products, arithmetic and copies ran while one was open for 11% of the time, Pallas kernels for 40%

profile of v2, /device:TPU:0, one launch (start us, length us, event | category | flops | bytes accessed | tf_op | source)
XLA Modules:
  0.0 496.8 jit_solution(16258267770546281502)
XLA Ops:
  7.8 3.5 send.1
  14.4 7.2 %collective-permute-done.3.refs_3_ = bf16[32,4736]{1,0:T(8,128)(2,1)S(1)} collective-permute-done((bf16[32,4736]{1,0:T(8,128)(2,1)}, bf16[32,4736]{1,0:T(8,128)(2,1)S(1)}, u32[]{:S(2)}, u32[]{:S(2)}) %collective-permute-start.3) | collective-permute-done | bytes 303136 | tf_op jit(solution)/shard_map/ppermute | solution.py:74
  21.6 6.5 %collective-permute-done.2.refs_2_ = bf16[32,4736]{1,0:T(8,128)(2,1)S(1)} collective-permute-done((bf16[32,4736]{1,0:T(8,128)(2,1)}, bf16[32,4736]{1,0:T(8,128)(2,1)S(1)}, u32[]{:S(2)}, u32[]{:S(2)}) %collective-permute-start.2) | collective-permute-done | bytes 303136 | tf_op jit(solution)/shard_map/ppermute | solution.py:74
  28.9 3.0 take.1
  31.9 3.4 collective-permute-start.6
  38.3 9.4 %collective-permute-done.6.refs_4_.refs_9_ = bf16[128,1024]{1,0:T(8,128)(2,1)S(1)} collective-permute-done((bf16[128,1024]{1,0:T(8,128)(2,1)}, bf16[128,1024]{1,0:T(8,128)(2,1)S(1)}, u32[]{:S(2)}, u32[]{:S(2)}) %collective-permute-start.6) | collective-permute-done | bytes 262176 | tf_op jit(solution)/shard_map/ppermute | solution.py:74
  49.1 6.3 %collective-permute-done.7.refs_6_.refs_11_ = bf16[128,1024]{1,0:T(8,128)(2,1)S(1)} collective-permute-done((bf16[128,1024]{1,0:T(8,128)(2,1)S(1)}, bf16[128,1024]{1,0:T(8,128)(2,1)S(1)}, u32[]{:S(2)}, u32[]{:S(2)}) %collective-permute-start.7) | collective-permute-done | bytes 262176 | tf_op jit(solution)/shard_map/ppermute | solution.py:74
  60.4 14.7 %collective-permute-done.10.refs_5_.refs_10_ = bf16[128,1024]{1,0:T(8,128)(2,1)S(1)} collective-permute-done((bf16[128,1024]{1,0:T(8,128)(2,1)S(1)}, bf16[128,1024]{1,0:T(8,128)(2,1)S(1)}, u32[]{:S(2)}, u32[]{:S(2)}) %collective-permute-start.10) | collective-permute-done | bytes 262176 | tf_op jit(solution)/shard_map/ppermute | solution.py:74
  75.1 8.2 %collective-permute-done.11.refs_7_.refs_12_ = bf16[128,1024]{1,0:T(8,128)(2,1)S(1)} collective-permute-done((bf16[128,1024]{1,0:T(8,128)(2,1)S(1)}, bf16[128,1024]{1,0:T(8,128)(2,1)S(1)}, u32[]{:S(2)}, u32[]{:S(2)}) %collective-permute-start.11) | collective-permute-done | bytes 262176 | tf_op jit(solution)/shard_map/ppermute | solution.py:74
  83.3 7.1 %collective-permute-done.4.refs_2_.refs_6_ = bf16[768,1024]{1,0:T(8,128)(2,1)} collective-permute-done((bf16[768,1024]{1,0:T(8,128)(2,1)S(1)}, bf16[768,1024]{1,0:T(8,128)(2,1)}, u32[]{:S(2)}, u32[]{:S(2)}) %collective-permute-start.4) | collective-permute-done | bytes 1572896 | tf_op jit(solution)/shard_map/ppermute | solution.py:74
  91.3 2.6 stack.13.refs_9_
  95.1 17.1 %mixer_in.1 = (bf16[3072,1024]{1,0:T(8,128)(2,1)}, f32[3072,768]{1,0:T(8,128)}, f32[3072,256]{1,0:T(8,128)}, bf16[3072,256]{1,0:T(8,128)(2,1)}, bf16[1024,768]{1,0:T(8,128)(2,1)}) custom-call(s32[4]{0:T(128)} %pad_add_fusion.where, bf16[768,1024]{1,0:T(8,128)(2,1)} %tokens.1, bf16[768,1024]{1,0:T(8,128)(2,1)} %collective-permute-done.refs_1_.refs_5_, ...), custom_call_target="tpu_custom_call" | custom-call | flops 4831838 | bytes 25165 | tf_op jit(solution)/shard_map/mixer_in/pallas_call | solution.py:107
  116.0 33.1 %collective-permute-done.15.refs_6_ = bf16[3072,256]{1,0:T(8,128)(2,1)S(1)} collective-permute-done((bf16[3072,256]{1,0:T(8,128)(2,1)}, bf16[3072,256]{1,0:T(8,128)(2,1)S(1)}, u32[]{:S(2)}, u32[]{:S(2)}) %collective-permute-start.15) | collective-permute-done | bytes 1572896 | tf_op jit(solution)/shard_map/ppermute | solution.py:74
  152.6 19.2 %residual.1 = (bf16[3072,1024]{1,0:T(8,128)(2,1)}, f32[768,1024]{1,0:T(8,128)}, bf16[768,1024]{1,0:T(8,128)(2,1)}, bf16[1024,1024]{1,0:T(8,128)(2,1)}) custom-call(s32[4]{0:T(128)} %pad_add_fusion.where, bf16[768,1024]{1,0:T(8,128)(2,1)} %tokens.1, bf16[768,1024]{1,0:T(8,128)(2,1)} %collective-permute-done.refs_1_.refs_5_, ...), custom_call_target="tpu_custom_call" | custom-call | flops 6442450 | bytes 25165 | tf_op jit(solution)/shard_map/residual/pallas_call | solution.py:107
  171.9 35.3 %ffn_own.1 = (bf16[3072,1152]{1,0:T(8,128)(2,1)}, bf16[3072,1152]{1,0:T(8,128)(2,1)}, bf16[3072,1152]{1,0:T(8,128)(2,1)}, bf16[3072,1024]{1,0:T(8,128)(2,1)}, bf...) custom-call(s32[4]{0:T(128)} %pad_add_fusion.where, ...), custom_call_target="tpu_custom_call" | custom-call | flops 21743272 | bytes 30277 | tf_op jit(solution)/shard_map/ffn_own/pallas_call | solution.py:107
  207.8 3.8 collective-permute-done.22.refs_3_.refs_4_
  212.7 35.7 %ffn_far.1 = (bf16[3072,1152]{1,0:T(8,128)(2,1)}, bf16[3072,1152]{1,0:T(8,128)(2,1)}, bf16[3072,1152]{1,0:T(8,128)(2,1)}, bf16[3072,1024]{1,0:T(8,128)(2,1)}, bf...) custom-call(s32[4]{0:T(128)} %pad_add_fusion.where, ...), custom_call_target="tpu_custom_call", output_to_operand_aliasing={{0}: (7, {}), {1}: (8, {}), {2}: (9, {}), {3}: (10, {})} | custom-call | flops 21743272 | bytes 30277 | tf_op jit(solution)/shard_map/ffn_far/pallas_call | solution.py:107
  249.0 4.0 collective-permute-done.25
  256.2 12.7 %convolution_convert_fusion.2.mine_keep.mine_send = bf16[1024,1152]{1,0:T(8,128)(2,1)S(1)} fusion(bf16[3072,1024]{1,0:T(8,128)(2,1)} %get-tuple-element.153.refs_0_, bf16[3072,1152]{1,0:T(8,128)(2,1)} %get-tuple-element.175), kind=kOutput, calls=%fused_computation.2 | convolution fusion | flops 7248936960 | bytes 15728640 | tf_op jit(solution)/shard_map/dot_general | solution.py:37
  271.3 9.1 %convolution_convert_fusion.1.mine_keep.mine_send = bf16[1024,1152]{1,0:T(8,128)(2,1)S(1)} fusion(bf16[3072,1024]{1,0:T(8,128)(2,1)S(1)} %bitcast.63, bf16[3072,1152]{1,0:T(8,128)(2,1)S(1)} %bitcast.57), kind=kOutput, calls=%fused_computation.1 | convolution fusion | flops 7248936960 | bytes 15728640 | tf_op jit(solution)/shard_map/dot_general | solution.py:37
  282.7 9.0 %convolution_convert_fusion.mine_keep.mine_send = bf16[1024,1152]{1,0:T(8,128)(2,1)S(1)} fusion(bf16[3072,1024]{1,0:T(8,128)(2,1)S(1)} %bitcast.52, bf16[3072,1152]{1,0:T(8,128)(2,1)S(1)} %bitcast.59), kind=kOutput, calls=%fused_computation | convolution fusion | flops 7248936960 | bytes 15728640 | tf_op jit(solution)/shard_map/dot_general | solution.py:37
  291.9 9.5 %residual_back.1 = (f32[768,1024]{1,0:T(8,128)}, bf16[768,1024]{1,0:T(8,128)(2,1)}, f32[1,1024]{1,0:T(1,128)}, bf16[768,256]{1,0:T(8,128)(2,1)}, bf16[768,256]{1,0:T(8,128)(2,1)}, /*index=5*/bf16[768,512]{1,0:T(8,128)(2,1)}) custom-call(s32[4]{0:T(128)} %pad_add_fusion.where, bf16[768,1024]{1,0:T(8,128)(2,1)} %get-tuple-element.178.g0, ...), custom_call_target="tpu_custom_call" | custom-call | flops 1610612 | bytes 15728 | tf_op jit(solution)/shard_map/residual_back/pallas_call | solution.py:107
  302.6 6.2 %out_grad.1 = (bf16[1024,256]{1,0:T(8,128)(2,1)}, bf16[1024,256]{1,0:T(8,128)(2,1)}, bf16[1024,256]{1,0:T(8,128)(2,1)}, bf16[1024,256]{1,0:T(8,128)(2,1)}) custom-call(s32[4]{0:T(128)} %pad_add_fusion.where, bf16[768,1024]{1,0:T(8,128)(2,1)} %get-tuple-element.183.left, bf16[768,1024]{1,0:T(8,128)(2,1)} %get-tuple-element.184.right), custom_call_target="tpu_custom_call" | custom-call | flops 1610612 | bytes 4718 | tf_op jit(solution)/shard_map/out_grad/pallas_call | solution.py:107
  311.9 3.2 gate_pair.1
  315.1 9.4 %collective-permute-done.30.got_keep.got_send = bf16[4,128,1152]{2,1,0:T(8,128)(2,1)S(1)} collective-permute-done((bf16[4,128,1152]{2,1,0:T(8,128)(2,1)}, bf16[4,128,1152]{2,1,0:T(8,128)(2,1)S(1)}, u32[]{:S(2)}, u32[]{:S(2)}) %collective-permute-start.30) | collective-permute-done | bytes 1179680 | tf_op jit(solution)/shard_map/ppermute | solution.py:74
  325.5 3.4 down_pair.1
  335.4 19.1 %mixer_back.1 = (bf16[3072,768]{1,0:T(8,128)(2,1)}, f32[8,256]{1,0:T(8,128)}, f32[1,1024]{1,0:T(1,128)}, bf16[768,1024]{1,0:T(8,128)(2,1)}, bf16[768,1024]{1,0:T...) custom-call(s32[4]{0:T(128)} %pad_add_fusion.where, bf16[768,256]{1,0:T(8,128)(2,1)} %get-tuple-element.180.refs_0_, ...), custom_call_target="tpu_custom_call" | custom-call | flops 4831838 | bytes 31457 | tf_op jit(solution)/shard_map/mixer_back/pallas_call | solution.py:107
  356.9 13.1 %in_grad.1 = (bf16[4,128,1024]{2,1,0:T(8,128)(2,1)}, bf16[4,128,1024]{2,1,0:T(8,128)(2,1)}) custom-call(s32[4]{0:T(128)} %pad_add_fusion.where, bf16[3072,1024]{1,0:T(8,128)(2,1)} %get-tuple-element.165.refs_0_, bf16[3072,768]{1,0:T(8,128)(2,1)} %get-tuple-element.198.refs_1_, bf16[1024,256]{1,0:T(8,128)(2,1)} %add_convert_fusion.3.refs_2_), custom_call_target="tpu_custom_call" | custom-call | flops 4831838 | bytes 11010 | tf_op jit(solution)/shard_map/in_grad/pallas_call | solution.py:107
  370.7 3.3 add_convert_fusion.2
  376.3 2.8 gate_half.1
  379.1 3.7 collective-permute-start.41
  382.8 3.4 up_pair.1
  387.8 3.2 add_convert_fusion
  393.2 2.8 down_half.1
  396.3 13.6 %collective-permute-done.43 = bf16[1,128,1152]{2,1,0:T(8,128)(2,1)S(1)} collective-permute-done((bf16[1,128,1152]{2,1,0:T(8,128)(2,1)}, bf16[1,128,1152]{2,1,0:T(8,128)(2,1)S(1)}, u32[]{:S(2)}, u32[]{:S(2)}) %collective-permute-start.43) | collective-permute-done | bytes 294944 | tf_op jit(solution)/shard_map/ppermute | solution.py:74
  410.6 3.6 mixer_pair.1
  414.2 5.3 %collective-permute-start.46 = (bf16[2,128,1024]{2,1,0:T(8,128)(2,1)}, bf16[2,128,1024]{2,1,0:T(8,128)(2,1)}, u32[]{:S(2)}, u32[]{:S(2)}) collective-permute-start(bf16[2,128,1024]{2,1,0:T(8,128)(2,1)} %get-tuple-element.228), channel_id=1, source_target_pairs={{0,8},{4,12},{8,0},{12,4},{16,24},{20,28},{24,16},{28,20},{1,9},{5... | collective-permute-start | bytes 1572872 | tf_op jit(solution)/shard_map/ppermute | solution.py:74
  419.6 2.8 up_half.1
  422.8 14.2 %collective-permute-done.46.got = bf16[2,128,1024]{2,1,0:T(8,128)(2,1)} collective-permute-done((bf16[2,128,1024]{2,1,0:T(8,128)(2,1)}, bf16[2,128,1024]{2,1,0:T(8,128)(2,1)}, u32[]{:S(2)}, u32[]{:S(2)}) %collective-permute-start.46) | collective-permute-done | bytes 524320 | tf_op jit(solution)/shard_map/ppermute | solution.py:74
  436.9 2.7 mixer_half.1
  439.6 5.1 %add_add_fusion = f32[768,1024]{1,0:T(8,128)} fusion(f32[768,1024]{1,0:T(8,128)S(1)} %copy-done.5, bf16[768,1024]{1,0:T(8,128)(2,1)} %collective-permute-done.36, bf16[768,1024]{1,0:T(8,128)(2,1)} %collective-permute-done.20, bf16[768,1024]{1,0:T(8,128)(2,1)} %get-tuple-element.156), kind=kLoop, calls=%fused_computation.4 | loop fusion | flops 4718592 | bytes 11010048 | tf_op jit(solution)/shard_map/add | solution.py:964
  445.5 3.4 ffn_finish.1
  448.9 6.7 %tokens_grad.1 = f32[768,1024]{1,0:T(8,128)} custom-call(s32[4]{0:T(128)} %pad_add_fusion.where, bf16[768,1024]{1,0:T(8,128)(2,1)} %get-tuple-element.206.g0, bf16[768,1024]{1,0:T(8,128)(2,1)} %copy-done.11, bf16[768,1024]{1,0:T(8,128)(2,1)} %collective-permute-done.40.g2, bf16[768,1024]{1,0:T(8,128)(2,1)} %tokens.1, ...), custom_call_target="tpu_custom_call" | custom-call | bytes 12582 | tf_op jit(solution)/shard_map/tokens_grad/pallas_call | solution.py:107
  456.3 2.5 mixer_finish.1
  460.8 2.9 collective-permute-done.53
  471.4 2.7 collective-permute-start.59
  476.9 7.5 %ffn_adam.1 = (f32[3,32,4608]{2,1,0:T(8,128)}, f32[3,32,4608]{2,1,0:T(8,128)}, f32[3,32,4608]{2,1,0:T(8,128)}) custom-call(s32[4]{0:T(128)} %pad_add_fusion.where, bf16[3,32,1152]{2,1,0:T(8,128)(2,1)} %get-tuple-element.252.g0, bf16[3,32,1152]{2,1,0:T(8,128)(2,1)} %copy-done.37, bf16[3,32,1152]{2,1,0:T(8,128)(2,1)} %copy-done.36, ...), custom_call_target="tpu_custom_call" | custom-call | bytes 11501 | tf_op jit(solution)/shard_map/ffn_adam/pallas_call | solution.py:107
  485.8 3.8 mixer_adam.1
  (255 shorter events, 71.0 us)
Async XLA Ops:
  7.2 164.7 %all-gather.2.cloned.1.call-start = ((), (), s32[]{:S(2)}) async-start(), calls=%async_computation | async-start | bytes 7962624 | tf_op jit(solution)/shard_map/all_gather | solution.py:594
  11.3 10.3 %collective-permute-start.3 = (bf16[32,4736]{1,0:T(8,128)(2,1)}, bf16[32,4736]{1,0:T(8,128)(2,1)S(1)}, u32[]{:S(2)}, u32[]{:S(2)}) collective-permute-start(bf16[32,4736]{1,0:T(8,128)(2,1)} %get-tuple-element.137), channel_id=1, source_target_pairs={{0,3},{1,2},{2,1},{3,0},{4,7},{5,6},{6,5},{7,4},{8,11},{9,10},{10,... | collective-permute-start | bytes 909320 | tf_op jit(solution)/shard_map/ppermute | solution.py:74
  14.4 13.8 %collective-permute-start.2 = (bf16[32,4736]{1,0:T(8,128)(2,1)}, bf16[32,4736]{1,0:T(8,128)(2,1)S(1)}, u32[]{:S(2)}, u32[]{:S(2)}) collective-permute-start(bf16[32,4736]{1,0:T(8,128)(2,1)} %get-tuple-element.136), channel_id=1, source_target_pairs={{0,2},{1,3},{2,0},{3,1},{4,6},{5,7},{6,4},{7,5},{8,10},{9,11},{10,... | collective-permute-start | bytes 909320 | tf_op jit(solution)/shard_map/ppermute | solution.py:74
  31.9 15.8 %collective-permute-start.6 = (bf16[128,1024]{1,0:T(8,128)(2,1)}, bf16[128,1024]{1,0:T(8,128)(2,1)S(1)}, u32[]{:S(2)}, u32[]{:S(2)}) collective-permute-start(bf16[128,1024]{1,0:T(8,128)(2,1)} %bitcast.66), channel_id=1, source_target_pairs={{0,16},{4,20},{8,24},{12,28},{16,0},{20,4},{24,8},{28,12},{1,17},{... | collective-permute-start | bytes 786440 | tf_op jit(solution)/shard_map/ppermute | solution.py:74
  35.3 13.2 %collective-permute-start.8 = (bf16[128,1024]{1,0:T(8,128)(2,1)}, bf16[128,1024]{1,0:T(8,128)(2,1)S(1)}, u32[]{:S(2)}, u32[]{:S(2)}) collective-permute-start(bf16[128,1024]{1,0:T(8,128)(2,1)} %bitcast.67), channel_id=1, source_target_pairs={{0,4},{4,0},{8,12},{12,8},{16,20},{20,16},{24,28},{28,24},{1,5},{5... | collective-permute-start | bytes 786440 | tf_op jit(solution)/shard_map/ppermute | solution.py:74
  36.8 12.3 %collective-permute-start.5 = (bf16[128,1024]{1,0:T(8,128)(2,1)}, bf16[128,1024]{1,0:T(8,128)(2,1)S(1)}, u32[]{:S(2)}, u32[]{:S(2)}) collective-permute-start(bf16[128,1024]{1,0:T(8,128)(2,1)} %bitcast.68), channel_id=1, source_target_pairs={{0,8},{4,12},{8,0},{12,4},{16,24},{20,28},{24,16},{28,20},{1,9},{5... | collective-permute-start | bytes 786440 | tf_op jit(solution)/shard_map/ppermute | solution.py:74
  55.4 35.0 %collective-permute-start.4 = (bf16[768,1024]{1,0:T(8,128)(2,1)S(1)}, bf16[768,1024]{1,0:T(8,128)(2,1)}, u32[]{:S(2)}, u32[]{:S(2)}) collective-permute-start(bf16[768,1024]{1,0:T(8,128)(2,1)S(1)} %copy-done), channel_id=1, source_target_pairs={{0,2},{1,3},{2,0},{3,1},{4,6},{5,7},{6,4},{7,5},{8,10},{9,11},{10,... | collective-permute-start | bytes 4718600 | tf_op jit(solution)/shard_map/ppermute | solution.py:74
  56.9 18.2 %collective-permute-start.9 = (bf16[128,1024]{1,0:T(8,128)(2,1)S(1)}, bf16[128,1024]{1,0:T(8,128)(2,1)S(1)}, u32[]{:S(2)}, u32[]{:S(2)}) collective-permute-start(bf16[128,1024]{1,0:T(8,128)(2,1)S(1)} %collective-permute-done.5.refs_2_.refs_7_), channel_id=1, source_target_pairs={{0,4},{4,0},{8,12},{12,8},{16,20},{20,16},{24,28},{28,24},{1,5},{5... | collective-permute-start | bytes 786440 | tf_op jit(solution)/shard_map/ppermute | solution.py:74
  58.4 16.7 %collective-permute-start.10 = (bf16[128,1024]{1,0:T(8,128)(2,1)S(1)}, bf16[128,1024]{1,0:T(8,128)(2,1)S(1)}, u32[]{:S(2)}, u32[]{:S(2)}) collective-permute-start(bf16[128,1024]{1,0:T(8,128)(2,1)S(1)} %collective-permute-done.6.refs_4_.refs_9_), channel_id=1, source_target_pairs={{0,4},{4,0},{8,12},{12,8},{16,20},{20,16},{24,28},{28,24},{1,5},{5... | collective-permute-start | bytes 786440 | tf_op jit(solution)/shard_map/ppermute | solution.py:74
  58.9 24.4 %collective-permute-start.11 = (bf16[128,1024]{1,0:T(8,128)(2,1)S(1)}, bf16[128,1024]{1,0:T(8,128)(2,1)S(1)}, u32[]{:S(2)}, u32[]{:S(2)}) collective-permute-start(bf16[128,1024]{1,0:T(8,128)(2,1)S(1)} %collective-permute-done.7.refs_6_.refs_11_), channel_id=1, source_target_pairs={{0,4},{4,0},{8,12},{12,8},{16,20},{20,16},{24,28},{28,24},{1,5},{5... | collective-permute-start | bytes 786440 | tf_op jit(solution)/shard_map/ppermute | solution.py:74
  60.4 34.7 %collective-permute-start = (bf16[768,1024]{1,0:T(8,128)(2,1)S(1)}, bf16[768,1024]{1,0:T(8,128)(2,1)}, u32[]{:S(2)}, u32[]{:S(2)}) collective-permute-start(bf16[768,1024]{1,0:T(8,128)(2,1)S(1)} %copy-done), channel_id=1, source_target_pairs={{0,1},{1,0},{2,3},{3,2},{4,5},{5,4},{6,7},{7,6},{8,9},{9,8},{10,11... | collective-permute-start | bytes 4718600 | tf_op jit(solution)/shard_map/ppermute | solution.py:74
  93.9 18.3 %collective-permute-start.13 = (bf16[1024,256]{1,0:T(8,128)(2,1)}, bf16[1024,256]{1,0:T(8,128)(2,1)}, u32[]{:S(2)}, u32[]{:S(2)}) collective-permute-start(bf16[1024,256]{1,0:T(8,128)(2,1)} %stack.13.refs_9_), channel_id=1, source_target_pairs={{0,2},{1,3},{2,0},{3,1},{4,6},{5,7},{6,4},{7,5},{8,10},{9,11},{10,... | collective-permute-start | bytes 1572872 | tf_op jit(solution)/shard_map/ppermute | solution.py:74
  112.2 36.8 %collective-permute-start.15 = (bf16[3072,256]{1,0:T(8,128)(2,1)}, bf16[3072,256]{1,0:T(8,128)(2,1)S(1)}, u32[]{:S(2)}, u32[]{:S(2)}) collective-permute-start(bf16[3072,256]{1,0:T(8,128)(2,1)} %get-tuple-element.150.refs_4_), channel_id=1, source_target_pairs={{0,2},{1,3},{2,0},{3,1},{4,6},{5,7},{6,4},{7,5},{8,10},{9,11},{10,... | collective-permute-start | bytes 4718600 | tf_op jit(solution)/shard_map/ppermute | solution.py:74
  113.6 36.8 %collective-permute-start.14 = (bf16[3072,256]{1,0:T(8,128)(2,1)}, bf16[3072,256]{1,0:T(8,128)(2,1)S(1)}, u32[]{:S(2)}, u32[]{:S(2)}) collective-permute-start(bf16[3072,256]{1,0:T(8,128)(2,1)} %get-tuple-element.150.refs_4_), channel_id=1, source_target_pairs={{0,1},{1,0},{2,3},{3,2},{4,5},{5,4},{6,7},{7,6},{8,9},{9,8},{10,11... | collective-permute-start | bytes 4718600 | tf_op jit(solution)/shard_map/ppermute | solution.py:74
  149.1 22.8 %collective-permute-start.19 = (bf16[768,1024]{1,0:T(8,128)(2,1)S(1)}, bf16[768,1024]{1,0:T(8,128)(2,1)}, u32[]{:S(2)}, u32[]{:S(2)}) collective-permute-start(bf16[768,1024]{1,0:T(8,128)(2,1)S(1)} %copy-done.4), channel_id=1, source_target_pairs={{0,1},{1,0},{2,3},{3,2},{4,5},{5,4},{6,7},{7,6},{8,9},{9,8},{10,11... | collective-permute-start | bytes 4718600 | tf_op jit(solution)/shard_map/ppermute | solution.py:74
  149.7 57.5 %collective-permute-start.21 = (bf16[768,1024]{1,0:T(8,128)(2,1)S(1)}, bf16[768,1024]{1,0:T(8,128)(2,1)S(1)}, u32[]{:S(2)}, u32[]{:S(2)}) collective-permute-start(bf16[768,1024]{1,0:T(8,128)(2,1)S(1)} %copy-done.4), channel_id=1, source_target_pairs={{0,2},{1,3},{2,0},{3,1},{4,6},{5,7},{6,4},{7,5},{8,10},{9,11},{10,... | collective-permute-start | bytes 4718600 | tf_op jit(solution)/shard_map/ppermute | solution.py:74
  207.4 41.0 %collective-permute-start.24 = (bf16[768,1024]{1,0:T(8,128)(2,1)}, bf16[768,1024]{1,0:T(8,128)(2,1)}, u32[]{:S(2)}, u32[]{:S(2)}) collective-permute-start(bf16[768,1024]{1,0:T(8,128)(2,1)} %get-tuple-element.173), channel_id=1, source_target_pairs={{0,1},{1,0},{2,3},{3,2},{4,5},{5,4},{6,7},{7,6},{8,9},{9,8},{10,11... | collective-permute-start | bytes 4718600 | tf_op jit(solution)/shard_map/ppermute | solution.py:74
  248.6 43.0 %collective-permute-start.20 = (bf16[768,1024]{1,0:T(8,128)(2,1)}, bf16[768,1024]{1,0:T(8,128)(2,1)}, u32[]{:S(2)}, u32[]{:S(2)}) collective-permute-start(bf16[768,1024]{1,0:T(8,128)(2,1)} %get-tuple-element.157), channel_id=1, source_target_pairs={{0,1},{1,0},{2,3},{3,2},{4,5},{5,4},{6,7},{7,6},{8,9},{9,8},{10,11... | collective-permute-start | bytes 4718600 | tf_op jit(solution)/shard_map/ppermute | solution.py:74
  255.3 36.6 %collective-permute-start.26 = (bf16[768,1024]{1,0:T(8,128)(2,1)S(1)}, bf16[768,1024]{1,0:T(8,128)(2,1)}, u32[]{:S(2)}, u32[]{:S(2)}) collective-permute-start(bf16[768,1024]{1,0:T(8,128)(2,1)S(1)} %add_convert_fusion.1), channel_id=1, source_target_pairs={{0,2},{1,3},{2,0},{3,1},{4,6},{5,7},{6,4},{7,5},{8,10},{9,11},{10,... | collective-permute-start | bytes 4718600 | tf_op jit(solution)/shard_map/ppermute | solution.py:74
  270.1 40.3 %collective-permute-start.29 = (bf16[4,128,1152]{2,1,0:T(8,128)(2,1)}, bf16[4,128,1152]{2,1,0:T(8,128)(2,1)}, u32[]{:S(2)}, u32[]{:S(2)}) collective-permute-start(bf16[4,128,1152]{2,1,0:T(8,128)(2,1)} %dynamic-slice_bitcast_fusion.2), channel_id=1, source_target_pairs={{0,4},{4,0},{8,12},{12,8},{16,20},{20,16},{24,28},{28,24},{1,5},{5... | collective-permute-start | bytes 3538952 | tf_op jit(solution)/shard_map/ppermute | solution.py:74
  281.8 42.7 %collective-permute-start.30 = (bf16[4,128,1152]{2,1,0:T(8,128)(2,1)}, bf16[4,128,1152]{2,1,0:T(8,128)(2,1)S(1)}, u32[]{:S(2)}, u32[]{:S(2)}) collective-permute-start(bf16[4,128,1152]{2,1,0:T(8,128)(2,1)} %dynamic-slice_bitcast_fusion.1), channel_id=1, source_target_pairs={{0,4},{4,0},{8,12},{12,8},{16,20},{20,16},{24,28},{28,24},{1,5},{5... | collective-permute-start | bytes 3538952 | tf_op jit(solution)/shard_map/ppermute | solution.py:74
  301.4 27.5 %collective-permute-start.28 = (bf16[768,512]{1,0:T(8,128)(2,1)}, bf16[768,512]{1,0:T(8,128)(2,1)}, u32[]{:S(2)}, u32[]{:S(2)}) collective-permute-start(bf16[768,512]{1,0:T(8,128)(2,1)} %get-tuple-element.182), channel_id=1, source_target_pairs={{0,2},{1,3},{2,0},{3,1},{4,6},{5,7},{6,4},{7,5},{8,10},{9,11},{10,... | collective-permute-start | bytes 2359304 | tf_op jit(solution)/shard_map/ppermute | solution.py:74
  302.6 21.9 %collective-permute-start.27 = (bf16[768,256]{1,0:T(8,128)(2,1)}, bf16[768,256]{1,0:T(8,128)(2,1)}, u32[]{:S(2)}, u32[]{:S(2)}) collective-permute-start(bf16[768,256]{1,0:T(8,128)(2,1)} %get-tuple-element.181), channel_id=1, source_target_pairs={{0,1},{1,0},{2,3},{3,2},{4,5},{5,4},{6,7},{7,6},{8,9},{9,8},{10,11... | collective-permute-start | bytes 1179656 | tf_op jit(solution)/shard_map/ppermute | solution.py:74
  308.8 21.7 %collective-permute-start.33 = (bf16[1024,256]{1,0:T(8,128)(2,1)}, bf16[1024,256]{1,0:T(8,128)(2,1)S(1)}, u32[]{:S(2)}, u32[]{:S(2)}) collective-permute-start(bf16[1024,256]{1,0:T(8,128)(2,1)} %get-tuple-element.201), channel_id=1, source_target_pairs={{0,1},{1,0},{2,3},{3,2},{4,5},{5,4},{6,7},{7,6},{8,9},{9,8},{10,11... | collective-permute-start | bytes 1572872 | tf_op jit(solution)/shard_map/ppermute | solution.py:74
  310.4 44.0 %collective-permute-start.35 = (bf16[4,128,1152]{2,1,0:T(8,128)(2,1)}, bf16[4,128,1152]{2,1,0:T(8,128)(2,1)S(1)}, u32[]{:S(2)}, u32[]{:S(2)}) collective-permute-start(bf16[4,128,1152]{2,1,0:T(8,128)(2,1)} %dynamic-slice_bitcast_fusion), channel_id=1, source_target_pairs={{0,4},{4,0},{8,12},{12,8},{16,20},{20,16},{24,28},{28,24},{1,5},{5... | collective-permute-start | bytes 3538952 | tf_op jit(solution)/shard_map/ppermute | solution.py:74
  330.0 24.5 %collective-permute-start.32 = (bf16[1024,256]{1,0:T(8,128)(2,1)}, bf16[1024,256]{1,0:T(8,128)(2,1)S(1)}, u32[]{:S(2)}, u32[]{:S(2)}) collective-permute-start(bf16[1024,256]{1,0:T(8,128)(2,1)} %get-tuple-element.199), channel_id=1, source_target_pairs={{0,1},{1,0},{2,3},{3,2},{4,5},{5,4},{6,7},{7,6},{8,9},{9,8},{10,11... | collective-permute-start | bytes 1572872 | tf_op jit(solution)/shard_map/ppermute | solution.py:74
  331.7 22.8 %collective-permute-start.34 = (bf16[1024,256]{1,0:T(8,128)(2,1)S(1)}, bf16[1024,256]{1,0:T(8,128)(2,1)}, u32[]{:S(2)}, u32[]{:S(2)}) collective-permute-start(bf16[1024,256]{1,0:T(8,128)(2,1)S(1)} %add_convert_fusion.4), channel_id=1, source_target_pairs={{0,2},{1,3},{2,0},{3,1},{4,6},{5,7},{6,4},{7,5},{8,10},{9,11},{10,... | collective-permute-start | bytes 1572872 | tf_op jit(solution)/shard_map/ppermute | solution.py:74
  332.9 37.7 %collective-permute-start.38 = (bf16[2,128,1152]{2,1,0:T(8,128)(2,1)}, bf16[2,128,1152]{2,1,0:T(8,128)(2,1)S(1)}, u32[]{:S(2)}, u32[]{:S(2)}) collective-permute-start(bf16[2,128,1152]{2,1,0:T(8,128)(2,1)} %get-tuple-element.212), channel_id=1, source_target_pairs={{0,8},{4,12},{8,0},{12,4},{16,24},{20,28},{24,16},{28,20},{1,9},{5... | collective-permute-start | bytes 1769480 | tf_op jit(solution)/shard_map/ppermute | solution.py:74
  335.4 35.3 %collective-permute-start.23 = (bf16[768,1024]{1,0:T(8,128)(2,1)}, bf16[768,1024]{1,0:T(8,128)(2,1)}, u32[]{:S(2)}, u32[]{:S(2)}) collective-permute-start(bf16[768,1024]{1,0:T(8,128)(2,1)} %get-tuple-element.164), channel_id=1, source_target_pairs={{0,1},{1,0},{2,3},{3,2},{4,5},{5,4},{6,7},{7,6},{8,9},{9,8},{10,11... | collective-permute-start | bytes 4718600 | tf_op jit(solution)/shard_map/ppermute | solution.py:74
  370.0 9.0 %collective-permute-start.37 = (bf16[768,1024]{1,0:T(8,128)(2,1)}, bf16[768,1024]{1,0:T(8,128)(2,1)S(1)}, u32[]{:S(2)}, u32[]{:S(2)}) collective-permute-start(bf16[768,1024]{1,0:T(8,128)(2,1)} %get-tuple-element.208), channel_id=1, source_target_pairs={{0,1},{1,0},{2,3},{3,2},{4,5},{5,4},{6,7},{7,6},{8,9},{9,8},{10,11... | collective-permute-start | bytes 4718600 | tf_op jit(solution)/shard_map/ppermute | solution.py:74
  370.6 15.6 %collective-permute-start.39 = (bf16[768,1024]{1,0:T(8,128)(2,1)}, bf16[768,1024]{1,0:T(8,128)(2,1)}, u32[]{:S(2)}, u32[]{:S(2)}) collective-permute-start(bf16[768,1024]{1,0:T(8,128)(2,1)} %get-tuple-element.213), channel_id=1, source_target_pairs={{0,1},{1,0},{2,3},{3,2},{4,5},{5,4},{6,7},{7,6},{8,9},{9,8},{10,11... | collective-permute-start | bytes 4718600 | tf_op jit(solution)/shard_map/ppermute | solution.py:74
  370.7 22.3 %collective-permute-start.42 = (bf16[2,128,1152]{2,1,0:T(8,128)(2,1)}, bf16[2,128,1152]{2,1,0:T(8,128)(2,1)}, u32[]{:S(2)}, u32[]{:S(2)}) collective-permute-start(bf16[2,128,1152]{2,1,0:T(8,128)(2,1)} %get-tuple-element.219), channel_id=1, source_target_pairs={{0,8},{4,12},{8,0},{12,4},{16,24},{20,28},{24,16},{28,20},{1,9},{5... | collective-permute-start | bytes 1769480 | tf_op jit(solution)/shard_map/ppermute | solution.py:74
  374.1 45.5 %collective-permute-start.36 = (bf16[768,1024]{1,0:T(8,128)(2,1)}, bf16[768,1024]{1,0:T(8,128)(2,1)}, u32[]{:S(2)}, u32[]{:S(2)}) collective-permute-start(bf16[768,1024]{1,0:T(8,128)(2,1)} %add_convert_fusion.2), channel_id=1, source_target_pairs={{0,2},{1,3},{2,0},{3,1},{4,6},{5,7},{6,4},{7,5},{8,10},{9,11},{10,... | collective-permute-start | bytes 4718600 | tf_op jit(solution)/shard_map/ppermute | solution.py:74
  374.8 35.8 %collective-permute-start.44 = (bf16[4,128,1024]{2,1,0:T(8,128)(2,1)}, bf16[4,128,1024]{2,1,0:T(8,128)(2,1)}, u32[]{:S(2)}, u32[]{:S(2)}) collective-permute-start(bf16[4,128,1024]{2,1,0:T(8,128)(2,1)} %get-tuple-element.223), channel_id=1, source_target_pairs={{0,4},{4,0},{8,12},{12,8},{16,20},{20,16},{24,28},{28,24},{1,5},{5... | collective-permute-start | bytes 3145736 | tf_op jit(solution)/shard_map/ppermute | solution.py:74
  379.1 17.2 %collective-permute-start.41 = (bf16[1,128,1152]{2,1,0:T(8,128)(2,1)}, bf16[1,128,1152]{2,1,0:T(8,128)(2,1)S(1)}, u32[]{:S(2)}, u32[]{:S(2)}) collective-permute-start(bf16[1,128,1152]{2,1,0:T(8,128)(2,1)} %get-tuple-element.218), channel_id=1, source_target_pairs={{0,16},{4,20},{8,24},{12,28},{16,0},{20,4},{24,8},{28,12},{1,17},{... | collective-permute-start | bytes 884744 | tf_op jit(solution)/shard_map/ppermute | solution.py:74
  386.3 27.9 %collective-permute-start.45 = (bf16[2,128,1152]{2,1,0:T(8,128)(2,1)}, bf16[2,128,1152]{2,1,0:T(8,128)(2,1)}, u32[]{:S(2)}, u32[]{:S(2)}) collective-permute-start(bf16[2,128,1152]{2,1,0:T(8,128)(2,1)} %get-tuple-element.227), channel_id=1, source_target_pairs={{0,8},{4,12},{8,0},{12,4},{16,24},{20,28},{24,16},{28,20},{1,9},{5... | collective-permute-start | bytes 1769480 | tf_op jit(solution)/shard_map/ppermute | solution.py:74
  393.0 55.9 %collective-permute-start.40 = (bf16[768,1024]{1,0:T(8,128)(2,1)}, bf16[768,1024]{1,0:T(8,128)(2,1)}, u32[]{:S(2)}, u32[]{:S(2)}) collective-permute-start(bf16[768,1024]{1,0:T(8,128)(2,1)} %add_convert_fusion), channel_id=1, source_target_pairs={{0,2},{1,3},{2,0},{3,1},{4,6},{5,7},{6,4},{7,5},{8,10},{9,11},{10,... | collective-permute-start | bytes 4718600 | tf_op jit(solution)/shard_map/ppermute | solution.py:74
  396.3 13.6 %collective-permute-start.43 = (bf16[1,128,1152]{2,1,0:T(8,128)(2,1)}, bf16[1,128,1152]{2,1,0:T(8,128)(2,1)S(1)}, u32[]{:S(2)}, u32[]{:S(2)}) collective-permute-start(bf16[1,128,1152]{2,1,0:T(8,128)(2,1)} %get-tuple-element.220), channel_id=1, source_target_pairs={{0,16},{4,20},{8,24},{12,28},{16,0},{20,4},{24,8},{28,12},{1,17},{... | collective-permute-start | bytes 884744 | tf_op jit(solution)/shard_map/ppermute | solution.py:74
  414.2 22.7 %collective-permute-start.46 = (bf16[2,128,1024]{2,1,0:T(8,128)(2,1)}, bf16[2,128,1024]{2,1,0:T(8,128)(2,1)}, u32[]{:S(2)}, u32[]{:S(2)}) collective-permute-start(bf16[2,128,1024]{2,1,0:T(8,128)(2,1)} %get-tuple-element.228), channel_id=1, source_target_pairs={{0,8},{4,12},{8,0},{12,4},{16,24},{20,28},{24,16},{28,20},{1,9},{5... | collective-permute-start | bytes 1572872 | tf_op jit(solution)/shard_map/ppermute | solution.py:74
  422.4 22.4 %collective-permute-start.47 = (bf16[1,128,1152]{2,1,0:T(8,128)(2,1)}, bf16[1,128,1152]{2,1,0:T(8,128)(2,1)S(1)}, u32[]{:S(2)}, u32[]{:S(2)}) collective-permute-start(bf16[1,128,1152]{2,1,0:T(8,128)(2,1)} %get-tuple-element.233), channel_id=1, source_target_pairs={{0,16},{4,20},{8,24},{12,28},{16,0},{20,4},{24,8},{28,12},{1,17},{... | collective-permute-start | bytes 884744 | tf_op jit(solution)/shard_map/ppermute | solution.py:74
  439.6 16.0 %collective-permute-start.48 = (bf16[1,128,1024]{2,1,0:T(8,128)(2,1)}, bf16[1,128,1024]{2,1,0:T(8,128)(2,1)S(1)}, u32[]{:S(2)}, u32[]{:S(2)}) collective-permute-start(bf16[1,128,1024]{2,1,0:T(8,128)(2,1)} %get-tuple-element.237), channel_id=1, source_target_pairs={{0,16},{4,20},{8,24},{12,28},{16,0},{20,4},{24,8},{28,12},{1,17},{... | collective-permute-start | bytes 786440 | tf_op jit(solution)/shard_map/ppermute | solution.py:74
  465.2 9.6 %collective-permute-start.56 = (bf16[3,32,1152]{2,1,0:T(8,128)(2,1)S(1)}, bf16[3,32,1152]{2,1,0:T(8,128)(2,1)S(1)}, u32[]{:S(2)}, u32[]{:S(2)}) collective-permute-start(bf16[3,32,1152]{2,1,0:T(8,128)(2,1)S(1)} %copy-done.52), channel_id=1, source_target_pairs={{0,2},{1,3},{2,0},{3,1},{4,6},{5,7},{6,4},{7,5},{8,10},{9,11},{10,... | collective-permute-start | bytes 663560 | tf_op jit(solution)/shard_map/ppermute | solution.py:74
  465.9 8.8 %collective-permute-start.55 = (bf16[3,32,1152]{2,1,0:T(8,128)(2,1)S(1)}, bf16[3,32,1152]{2,1,0:T(8,128)(2,1)S(1)}, u32[]{:S(2)}, u32[]{:S(2)}) collective-permute-start(bf16[3,32,1152]{2,1,0:T(8,128)(2,1)S(1)} %copy-done.51), channel_id=1, source_target_pairs={{0,1},{1,0},{2,3},{3,2},{4,5},{5,4},{6,7},{7,6},{8,9},{9,8},{10,11... | collective-permute-start | bytes 663560 | tf_op jit(solution)/shard_map/ppermute | solution.py:74
  466.0 10.3 %collective-permute-start.57 = (bf16[3,32,1152]{2,1,0:T(8,128)(2,1)S(1)}, bf16[3,32,1152]{2,1,0:T(8,128)(2,1)S(1)}, u32[]{:S(2)}, u32[]{:S(2)}) collective-permute-start(bf16[3,32,1152]{2,1,0:T(8,128)(2,1)S(1)} %copy-done.50), channel_id=1, source_target_pairs={{0,3},{1,2},{2,1},{3,0},{4,7},{5,6},{6,5},{7,4},{8,11},{9,10},{10,... | collective-permute-start | bytes 663560 | tf_op jit(solution)/shard_map/ppermute | solution.py:74
  471.4 13.0 %collective-permute-start.59 = (f32[5,256]{1,0:T(8,128)S(1)}, f32[5,256]{1,0:T(8,128)S(1)}, u32[]{:S(2)}, u32[]{:S(2)}) collective-permute-start(f32[5,256]{1,0:T(8,128)S(1)} %add.101), channel_id=1, source_target_pairs={{0,16},{4,20},{8,24},{12,28},{16,0},{20,4},{24,8},{28,12},{1,17},{... | collective-permute-start | bytes 15368 | tf_op jit(solution)/shard_map/ppermute | solution.py:74
  474.1 11.0 %collective-permute-start.50 = (bf16[1,32,1024]{2,1,0:T(8,128)(2,1)}, bf16[1,32,1024]{2,1,0:T(8,128)(2,1)S(1)}, u32[]{:S(2)}, u32[]{:S(2)}) collective-permute-start(bf16[1,32,1024]{2,1,0:T(8,128)(2,1)} %get-tuple-element.243), channel_id=1, source_target_pairs={{0,2},{1,3},{2,0},{3,1},{4,6},{5,7},{6,4},{7,5},{8,10},{9,11},{10,... | collective-permute-start | bytes 196616 | tf_op jit(solution)/shard_map/ppermute | solution.py:74
  474.8 10.3 %collective-permute-start.49 = (bf16[1,32,1024]{2,1,0:T(8,128)(2,1)}, bf16[1,32,1024]{2,1,0:T(8,128)(2,1)S(1)}, u32[]{:S(2)}, u32[]{:S(2)}) collective-permute-start(bf16[1,32,1024]{2,1,0:T(8,128)(2,1)} %get-tuple-element.241), channel_id=1, source_target_pairs={{0,1},{1,0},{2,3},{3,2},{4,5},{5,4},{6,7},{7,6},{8,9},{9,8},{10,11... | collective-permute-start | bytes 196616 | tf_op jit(solution)/shard_map/ppermute | solution.py:74
  474.8 10.3 %collective-permute-start.51 = (bf16[1,32,1024]{2,1,0:T(8,128)(2,1)}, bf16[1,32,1024]{2,1,0:T(8,128)(2,1)S(1)}, u32[]{:S(2)}, u32[]{:S(2)}) collective-permute-start(bf16[1,32,1024]{2,1,0:T(8,128)(2,1)} %get-tuple-element.244), channel_id=1, source_target_pairs={{0,3},{1,2},{2,1},{3,0},{4,7},{5,6},{6,5},{7,4},{8,11},{9,10},{10,... | collective-permute-start | bytes 196616 | tf_op jit(solution)/shard_map/ppermute | solution.py:74
  (74 other events, 1081.1 us)
Sparse Core Ops, SparseCore 0:
  55.5 112.3 all-gather.1
